TPU v7x, 128 devices: a whole 4x4x4 slice. The times are simulated.
128 devices in a mesh: slab: 16 (over x, z), sub: 8 (over y, core).
Axes of the slice: x: 4, y: 4, z: 4, core: 2. Of those that a mesh axis runs over, the one named last changes fastest.
Arguments:
- multipoles: bfloat16 [4096, 64, 512], P(('slab', 'sub')), may hold values from -6 to 6
- translations: bfloat16 [24, 512, 512], replicated, may hold values from -0.0546875 to 0.0546875
- local_source: int32 [16, 4096], P(None, ('slab', 'sub')), may hold values from 0 to 31
- remote_owner: int32 [32768, 1], P(('slab', 'sub')), may hold values from 0 to 127; in each aligned block of 256 rows (0 to 255, 256 to 511, ...) at most 2 rows name the same one
- remote_box: int32 [32768], P(('slab', 'sub')), may hold values from 0 to 31
- charges: bfloat16 [64, 262144], P(None, ('slab', 'sub')), may hold values from -6 to 6
- positions: float32 [3, 262144], P(None, ('slab', 'sub')), may hold values from -1 to 1
- leaf_count: int32 [4096], P(('slab', 'sub')), may hold values from 1 to 64
Outputs:
- expansion: float32 [4096, 64, 512], P(('slab', 'sub'))
- potential: float32 [64, 262144], P(None, ('slab', 'sub'))
Inputs may be any that keep to these rules, and one draw needn't show every extreme that they name: `remote_owner`: within the rows of one device, each source device number appears at most 2 times.
All inputs are finite; a program needn't handle non-finite values.
Results may differ from a plain program's by a relative error of at most 0.0003.
Values may be sent and summed in bfloat16 or wider, within the bound.
A program may use at most 256 MiB of HBM per device.

v0:
```python
import jax
import jax.numpy as jnp
from jax import lax
from jax.sharding import PartitionSpec as P

ORDER = 8
SLOTS = 64


length_factor = 1.7320508075688772


def extended(cells, sides, width):
    for axis, dim in sides:
        count = lax.axis_size(axis)
        ends = count - 1
        head = lax.slice_in_dim(cells, 0, width, axis=dim)
        tail = lax.slice_in_dim(cells, cells.shape[dim] - width, cells.shape[dim], axis=dim)
        cells = jnp.concatenate(
            [
                lax.ppermute(tail, axis, [(i, (i + 1) % count) for i in range(ends)]),
                cells,
                lax.ppermute(head, axis, [((i + 1) % count, i) for i in range(ends)]),
            ],
            axis=dim,
        )
    return cells


def node_weights(coord):
    steps = jnp.arange(ORDER).astype(jnp.float32)
    angles = (2.0 * steps + 1.0) * jnp.pi / (2.0 * ORDER)
    theta = jnp.arccos(coord)
    at_point = jnp.cos(theta[..., None] * steps)
    at_node = jnp.cos(angles[:, None] * steps[None, :])
    total = jnp.sum(at_point[..., None, :] * at_node, axis=-1)
    return (2.0 * total - 1.0) / ORDER


def interpolate(positions):
    first = node_weights(positions[0])
    second = node_weights(positions[1])
    third = node_weights(positions[2])
    table = first[:, :, None, None] * second[:, None, :, None] * third[:, None, None, :]
    return table.reshape(positions.shape[1], ORDER * ORDER * ORDER)


def near_field(padded, leaves):
    targets = padded[:3, 1 : leaves + 1]
    windows = jnp.stack([padded[:, o : o + leaves] for o in range(3)], axis=1)
    source_pos = jnp.transpose(windows[:3], (0, 2, 1, 3))
    diff = targets[:, :, :, None, None] - source_pos[:, :, None, :, :]
    offset = 2.0 * (jnp.arange(3).astype(jnp.float32) - 1.0)
    first = diff[0] - offset[None, None, :, None]
    dist = jnp.sqrt(first * first + diff[1] * diff[1] + diff[2] * diff[2])
    kernel = (1.0 + length_factor * dist) * jnp.exp(-length_factor * dist)
    return jnp.einsum("lqos,rols->rlq", kernel, windows[3:], precision=lax.Precision.HIGHEST)


def on_device(
    multipoles, translations, local_source, remote_owner, remote_box, charges, positions, leaf_count
):
    boxes, rhs, coefs = multipoles.shape
    devices = lax.axis_size(("slab", "sub"))
    local_types = local_source.shape[0]
    remote_rows = remote_box.shape[0]
    remote_types = remote_rows // boxes
    capacity = max(2, (remote_rows + devices - 1) // devices)
    local_blocks = jnp.take(multipoles, local_source.reshape(-1), axis=0).reshape(
        local_types, boxes, rhs, coefs
    )
    owner = remote_owner[:, 0]
    onehot = (owner[:, None] == jnp.arange(devices)[None, :]).astype(jnp.int32)
    before = jnp.cumsum(onehot, axis=0) - onehot
    rank = jnp.sum(before * onehot, axis=1)
    slot_index = owner * capacity + rank
    wanted = jnp.zeros((devices * capacity,), jnp.int32).at[slot_index].set(remote_box)
    asked = lax.all_to_all(
        wanted.reshape(devices, capacity), ("slab", "sub"), split_axis=0, concat_axis=0, tiled=True
    )
    served = jnp.take(multipoles, asked.reshape(-1), axis=0).reshape(devices, capacity, rhs, coefs)
    arrived = lax.all_to_all(served, ("slab", "sub"), split_axis=0, concat_axis=0, tiled=True)
    arrived = arrived.reshape(devices * capacity, rhs, coefs)
    remote_blocks = jnp.take(arrived, slot_index, axis=0).reshape(remote_types, boxes, rhs, coefs)
    sources = jnp.concatenate([local_blocks, remote_blocks], 0)
    expansion = jnp.einsum(
        "tbrp,tpq->brq", sources, translations, preferred_element_type=jnp.float32
    )
    present = (jnp.arange(SLOTS)[None, :] < leaf_count[:, None]).astype(jnp.float32)
    weights = interpolate(positions).reshape(boxes, SLOTS, coefs)
    far = jnp.einsum("brp,bqp->rbq", expansion, weights, precision=lax.Precision.HIGHEST)
    masked = charges.astype(jnp.float32).reshape(rhs, boxes, SLOTS) * present[None]
    packed = jnp.concatenate([positions.reshape(3, boxes, SLOTS), masked], 0)
    padded = extended(packed, ((("slab", "sub"), 1),), 1)
    near = near_field(padded, boxes)
    potential = ((near + far) * present[None]).reshape(rhs, boxes * SLOTS)
    return (expansion, potential)


def solution(mesh):
    placed = (
        P(("slab", "sub"), None, None),
        P(),
        P(None, ("slab", "sub")),
        P(("slab", "sub"), None),
        P(("slab", "sub")),
        P(None, ("slab", "sub")),
        P(None, ("slab", "sub")),
        P(("slab", "sub")),
    )
    return jax.shard_map(
        on_device,
        mesh=mesh,
        in_specs=placed,
        out_specs=(P(("slab", "sub"), None, None), P(None, ("slab", "sub"))),
        check_vma=False,
    )
```

profile of v0, /device:TPU:98, one launch (start us, length us, event | category | flops | bytes accessed | tf_op | source)
XLA Modules:
  0.0 377.1 jit_solution(7296064191873563846)
XLA Ops:
  0.6 0.9 copy.49
  1.9 0.9 fusion.50
  2.7 0.7 and_reduce_fusion
  3.5 1.6 scatter_custom_fusion
  5.2 16.0 %all_to_all.14 = s32[128,1,2]{2,1,0:T(1,128)S(1)} all-to-all(s32[128,1,2]{2,1,0:T(1,128)S(1)} %bitcast.105), channel_id=1, replica_groups=mesh['slab'=16,'sub'=8] {'slab','sub'}, dimensions={0} | all-to-all | bytes 2048 | tf_op jit(solution)/shard_map/all_to_all | solution.py:78
  21.2 0.5 broadcast.338
  21.7 0.8 reduce.5
  22.7 9.7 %gather_fusion.1 = bf16[256,64,512]{2,1,0:T(8,128)(2,1)} fusion(bf16[32,64,512]{2,1,0:T(8,128)(2,1)S(1)} %copy-done, s32[1024]{0:T(1024)S(1)} %pad_clamp_fusion.1), kind=kCustom, calls=%fused_computation.1 | custom fusion | bytes 33555456 | tf_op jit(solution)/shard_map/jit(_take)/gather | solution.py:81
  32.5 14.2 %broadcast_select_fusion = bf16[128,2,64,512]{3,2,1,0:T(8,128)(2,1)} fusion(bf16[128,2,64,512]{3,2,1,0:T(8,128)(2,1)} %bitcast.101, pred[128,2]{1,0:T(8,128)(4,1)S(1)} %compare_and_fusion), kind=kLoop, calls=%fused_computation.10 | loop fusion | flops 8388608 | bytes 33554688 | tf_op jit(solution)/shard_map/jit(_take)/select_n | solution.py:81
  46.6 9.0 %all-to-all-start.1 = ((bf16[128,2,64,512]{3,2,1,0:T(8,128)(2,1)}), bf16[128,2,64,512]{3,2,1,0:T(8,128)(2,1)}, u32[]{:S(2)}, u32[]{:S(2)}) async-start(bf16[128,2,64,512]{3,2,1,0:T(8,128)(2,1)} %broadcast_select_fusion), calls=%async_computation.1 | async-start | bytes 33554432 | tf_op jit(solution)/shard_map/all_to_all | solution.py:82
  55.7 1.5 reshape.353
  57.4 1.8 copy_multiply_fusion
  59.2 2.1 collective-permute-start
  61.3 5.6 %collective-permute-start.1 = (f32[67,1,64]{2,0,1:T(8,128)S(1)}, f32[67,1,64]{2,0,1:T(8,128)S(1)}, u32[]{:S(2)}, u32[]{:S(2)}) collective-permute-start(f32[67,1,64]{2,0,1:T(8,128)S(1)} %get-tuple-element.11), channel_id=1, source_target_pairs={{1,0},{2,1},{3,2},{4,3},{5,4},{6,5},{7,6},{8,7},{9,8},{10,9},{11,1... | collective-permute-start | bytes 51464 | tf_op jit(solution)/shard_map/ppermute | solution.py:23
  67.0 16.3 %gather_fusion = bf16[512,64,512]{2,1,0:T(8,128)(2,1)} fusion(bf16[32,64,512]{2,1,0:T(8,128)(2,1)S(1)} %copy-done, s32[1024]{0:T(1024)S(1)} %pad_clamp_fusion.2), kind=kCustom, calls=%fused_computation | custom fusion | bytes 67110912 | tf_op jit(solution)/shard_map/jit(_take)/gather | solution.py:69
  83.7 0.7 multiply_cosine_fusion
  84.4 0.5 multiply_reduce_fusion.2
  85.0 2.6 broadcast_multiply_fusion
  87.7 22.9 %copy_select_fusion = bf16[16,32,64,512]{3,2,0,1:T(8,128)(2,1)} fusion(bf16[16,32,64,512]{3,2,1,0:T(8,128)(2,1)} %bitcast.99, pred[16,32]{0,1:T(8,128)(4,1)S(1)} %copy.47), kind=kLoop, calls=%fused_computation.8 | loop fusion | flops 16777216 | bytes 67109376 | tf_op jit(solution)/shard_map/jit(_take)/select_n | solution.py:69
  110.7 7.8 %mul.311 = f32[32,64,512]{1,0,2:T(8,128)} reshape(f32[2048,8,8,8]{0,3,2,1:T(8,128)} %broadcast_multiply_fusion) | data formatting | bytes 8388608 | tf_op jit(solution)/shard_map/mul | solution.py:44
  118.6 81.3 %collective-permute-done = f32[67,1,64]{2,0,1:T(8,128)S(1)} collective-permute-done((f32[67,1,64]{2,0,1:T(8,128)S(1)}, f32[67,1,64]{2,0,1:T(8,128)S(1)}, u32[]{:S(2)}, u32[]{:S(2)}) %collective-permute-start) | collective-permute-done | bytes 17184 | tf_op jit(solution)/shard_map/ppermute | solution.py:21
  199.9 14.0 %collective-permute-done.1 = f32[67,1,64]{2,0,1:T(8,128)S(1)} collective-permute-done((f32[67,1,64]{2,0,1:T(8,128)S(1)}, f32[67,1,64]{2,0,1:T(8,128)S(1)}, u32[]{:S(2)}, u32[]{:S(2)}) %collective-permute-start.1) | collective-permute-done | bytes 17184 | tf_op jit(solution)/shard_map/ppermute | solution.py:23
  214.3 0.3 pad_maximum_fusion
  214.7 1.6 broadcast_subtract_fusion
  216.3 6.0 %fusion.40 = f32[64,32,64]{2,0,1:T(8,128)S(1)} fusion(f32[3,32,64,3,64]{4,2,3,1,0:T(8,128)S(1)} %broadcast_subtract_fusion, f32[3]{0:T(128)S(1)} %add_multiply_fusion.4, f32[67,3,32,64]{3,0,1,2:T(8,128)S(1)} %pad_maximum_fusion), kind=kOutput, calls=%fused_computation.45 | convolution fusion | flops 305922048 | bytes 13107712 | tf_op jit(solution)/shard_map/lqos,rols->rlq/dot_general | solution.py:57
  222.3 75.2 %all-to-all-done.1 = bf16[128,2,64,512]{3,2,1,0:T(8,128)(2,1)} async-done(((bf16[128,2,64,512]{3,2,1,0:T(8,128)(2,1)}), bf16[128,2,64,512]{3,2,1,0:T(8,128)(2,1)}, u32[]{:S(2)}, u32[]{:S(2)}) %all-to-all-start.1) | async-done | bytes 16777248 | tf_op jit(solution)/shard_map/all_to_all | solution.py:82
  297.5 15.8 %gather_fusion.2 = bf16[256,64,512]{2,1,0:T(8,128)(2,1)} fusion(bf16[256,64,512]{2,1,0:T(8,128)(2,1)} %bitcast.13, s32[1024]{0:T(1024)S(1)} %pad_clamp_fusion), kind=kCustom, calls=%fused_computation.2 | custom fusion | bytes 33555456 | tf_op jit(solution)/shard_map/jit(_take)/gather | solution.py:84
  313.2 14.1 %copy_select_fusion.1 = bf16[8,32,64,512]{3,2,0,1:T(8,128)(2,1)} fusion(bf16[8,32,64,512]{3,2,1,0:T(8,128)(2,1)} %bitcast.100, pred[8,32]{0,1:T(8,128)(4,1)S(1)} %copy.51), kind=kLoop, calls=%fused_computation.9 | loop fusion | flops 8388608 | bytes 33554688 | tf_op jit(solution)/shard_map/jit(_take)/select_n | solution.py:84
  327.4 35.8 %fusion.22 = f32[32,64,512]{2,1,0:T(8,128)} fusion(bf16[24,512,512]{2,1,0:T(8,128)(2,1)} %param.9, bf16[8,32,64,512]{3,2,0,1:T(8,128)(2,1)} %copy_select_fusion.1, bf16[16,32,64,512]{3,2,0,1:T(8,128)(2,1)} %copy_select_fusion), kind=kOutput, calls=%fused_computation.33 | convolution fusion | flops 25794969600 | bytes 67108864 | tf_op jit(solution)/shard_map/tbrp,tpq->brq/dot_general | solution.py:86
  363.2 12.1 %fusion.37 = f32[64,32,64]{2,0,1:T(8,128)S(1)} fusion(f32[64,32,64]{2,0,1:T(8,128)S(1)} %fusion.40, f32[32,64,512]{2,1,0:T(8,128)} %fusion.22, f32[32,64,512]{1,0,2:T(8,128)} %mul.311, f32[32,64]{1,0:T(8,128)S(1)} %fusion.55), kind=kOutput, calls=%fused_computation.44 | convolution fusion | flops 805568512 | bytes 9445376 | tf_op jit(solution)/shard_map/brp,bqp->rbq/dot_general | solution.py:91
  375.4 0.6 copy.61
  376.0 1.2 reshape.351
  (50 shorter events, 1.8 us)
Async XLA Ops:
  0.6 22.1 %copy-start = (bf16[32,64,512]{2,1,0:T(8,128)(2,1)S(1)}, bf16[32,64,512]{2,1,0:T(8,128)(2,1)}, u32[]{:S(2)}) copy-start(bf16[32,64,512]{2,1,0:T(8,128)(2,1)} %param.8) | copy-start | bytes 6291460
  46.6 9.0 %copy-start.2 = (bf16[64,2048]{1,0:T(8,128)(2,1)S(1)}, bf16[64,2048]{1,0:T(8,128)(2,1)}, u32[]{:S(2)}) copy-start(bf16[64,2048]{1,0:T(8,128)(2,1)} %param.13) | copy-start | bytes 786436
  46.6 10.5 %copy-start.3 = (f32[3,2048]{1,0:T(4,128)S(1)}, f32[3,2048]{1,0:T(4,128)}, u32[]{:S(2)}) copy-start(f32[3,2048]{1,0:T(4,128)} %param.14) | copy-start | bytes 73732
  46.6 10.7 %copy-start.5 = (s32[32]{0:T(128)S(1)}, s32[32]{0:T(128)}, u32[]{:S(2)}) copy-start(s32[32]{0:T(128)} %param.15) | copy-start | bytes 388
  46.6 250.8 %all-to-all-start.1 = ((bf16[128,2,64,512]{3,2,1,0:T(8,128)(2,1)}), bf16[128,2,64,512]{3,2,1,0:T(8,128)(2,1)}, u32[]{:S(2)}, u32[]{:S(2)}) async-start(bf16[128,2,64,512]{3,2,1,0:T(8,128)(2,1)} %broadcast_select_fusion), calls=%async_computation.1 | async-start | bytes 33554432 | tf_op jit(solution)/shard_map/all_to_all | solution.py:82
  55.7 11.2 %copy-start.4 = (s32[16,32]{1,0:T(8,128)S(1)}, s32[16,32]{1,0:T(8,128)}, u32[]{:S(2)}) copy-start(s32[16,32]{1,0:T(8,128)} %param.10) | copy-start | bytes 6148
  59.2 140.7 %collective-permute-start = (f32[67,1,64]{2,0,1:T(8,128)S(1)}, f32[67,1,64]{2,0,1:T(8,128)S(1)}, u32[]{:S(2)}, u32[]{:S(2)}) collective-permute-start(f32[67,1,64]{2,0,1:T(8,128)S(1)} %get-tuple-element.10), channel_id=1, source_target_pairs={{0,1},{1,2},{2,3},{3,4},{4,5},{5,6},{6,7},{7,8},{8,9},{9,10},{10,1... | collective-permute-start | bytes 51464 | tf_op jit(solution)/shard_map/ppermute | solution.py:21
  61.3 152.7 %collective-permute-start.1 = (f32[67,1,64]{2,0,1:T(8,128)S(1)}, f32[67,1,64]{2,0,1:T(8,128)S(1)}, u32[]{:S(2)}, u32[]{:S(2)}) collective-permute-start(f32[67,1,64]{2,0,1:T(8,128)S(1)} %get-tuple-element.11), channel_id=1, source_target_pairs={{1,0},{2,1},{3,2},{4,3},{5,4},{6,5},{7,6},{8,7},{9,8},{10,9},{11,1... | collective-permute-start | bytes 51464 | tf_op jit(solution)/shard_map/ppermute | solution.py:23
  363.2 13.9 %copy-start.1 = (bf16[32,64,512]{2,1,0:T(8,128)(2,1)S(1)}, bf16[32,64,512]{2,1,0:T(8,128)(2,1)}, u32[]{:S(2)}) copy-start(bf16[32,64,512]{2,1,0:T(8,128)(2,1)} %param.8) | copy-start | bytes 6291460
where the time goes:
time: 378 us; the launch traced here: 377 us
  waiting for transfers between devices  171 us (45%)
  other arithmetic  62.1 us (16%)
  local copies, waits for them, and re-layouts  56.8 us (15%)
  matrix products  54 us (14%)
  starting transfers between devices  16.7 us (4%)
  blocking collectives  16 us (4%)
    ppermute x1, waiting for transfers between devices, extended(): lax.ppermute(tail, axis, [(i, (i + 1) % count) for i in range(ends)])  81.3 us
    all_to_all x1, waiting for transfers between devices, on_device(): lax.all_to_all(served, ('slab', 'sub'), split_axis=0, concat_axis=0, tile...  75.2 us
    dot_general x1, matrix products, on_device(): jnp.einsum('tbrp,tpq->brq', sources, translations, preferred_element_type...  35.8 us
    select_n x2, other arithmetic, on_device(): jnp.take(multipoles, local_source.reshape(-1), axis=0)  22.9 us
    gather x1, local copies, waits for them, and re-layouts, on_device(): jnp.take(multipoles, local_source.reshape(-1), axis=0)  16.3 us
    all_to_all x1, blocking collectives, on_device(): lax.all_to_all(wanted.reshape(devices, capacity), ('slab', 'sub'), split_...  16 us
    gather x1, local copies, waits for them, and re-layouts, on_device(): jnp.take(arrived, slot_index, axis=0)  15.8 us
    select_n x2, other arithmetic, on_device(): jnp.take(multipoles, asked.reshape(-1), axis=0)  14.2 us
  transfers between devices with their start and end apart: 3, of which 3 were waited for; matrix products, arithmetic and copies ran while one was open for 17% of the time, Pallas kernels for 0%

commit v1 on v0

--- a/solution.py
+++ b/solution.py
@@ -1,13 +1,185 @@
 import jax
 import jax.numpy as jnp
 from jax import lax
+from jax.experimental import pallas as pl
+from jax.experimental.pallas import tpu as pltpu
 from jax.sharding import PartitionSpec as P
 
 ORDER = 8
 SLOTS = 64
-
-
-length_factor = 1.7320508075688772
+MESH = pl.DeviceIdType.MESH
+
+PARTS = ((0, 0, 0, 512), (1, 16, 0, 512), (2, 32, 0, 512), (0, 48, 0, 128), (1, 48, 128, 128), (2, 48, 256, 256))
+ORDERS = ("xyz", "yzx", "zxy")
+ROWS = 16
+
+
+def place(at, core):
+    return (at["x"] * 4 + at["z"], at["y"] * 2 + core)
+
+
+def index_of(at, core):
+    return at["x"] * 32 + at["z"] * 8 + at["y"] * 2 + core
+
+
+def moved(at, axis, step):
+    other = dict(at)
+    other[axis] = (at[axis] + step) % 4
+    return other
+
+
+def exchange_kernel(owner_ref, box_ref, mult_ref, f0, f1, f2, f3, f4, f5, *scratch):
+    finals = (f0, f1, f2, f3, f4, f5)
+    gathered, packed, relay = scratch[0:6], scratch[6:12], scratch[12:18]
+    ask_v, ask_s = scratch[18:20]
+    ask_send, ask_recv, copy_sem, g_send, g_recv, g_own, s_send, s_recv, f_send, f_recv, f_own = scratch[20:]
+    slab, sub = lax.axis_index("slab"), lax.axis_index("sub")
+    me = {"x": slab // 4, "y": sub // 2, "z": slab % 4}
+    core = sub % 2
+    mine = index_of(me, core)
+
+    barrier = pltpu.get_barrier_semaphore()
+    partners = [(me, 1 - core)]
+    for axis in "xyz":
+        for step in (1, 3, 2):
+            for other in (core, 1 - core):
+                partners.append((moved(me, axis, step), other))
+    for at, c in partners:
+        pl.semaphore_signal(barrier, 1, device_id=place(at, c), device_id_type=MESH)
+
+    owner, box = owner_ref[...], box_ref[...]
+    rows = owner.shape[0]
+    down = lax.broadcasted_iota(jnp.int32, (rows, rows), 0)
+    along = lax.broadcasted_iota(jnp.int32, (rows, rows), 1)
+    across = jnp.sum(jnp.where(down == along, owner, 0), axis=0, keepdims=True)
+    before = jnp.where((owner == across) & (along < down), 1, 0)
+    rank = jnp.sum(before, axis=1, keepdims=True)
+    named = owner == lax.broadcasted_iota(jnp.int32, (rows, 128), 1)
+    for r in range(2):
+        wanted = jnp.sum(jnp.where(named & (rank == r), box, 0), axis=0, keepdims=True)
+        ask_v[mine, r : r + 1, :] = wanted
+
+    pl.semaphore_wait(barrier, len(partners))
+
+    def send(src, dst, ssem, rsem, at, c):
+        pltpu.make_async_remote_copy(
+            src_ref=src, dst_ref=dst, send_sem=ssem, recv_sem=rsem, device_id=place(at, c), device_id_type=MESH
+        ).start()
+
+    def drain(ref, sem):
+        pltpu.make_async_copy(ref, ref, sem).wait()
+
+    for step in (0, 1, 3, 2):
+        for c in (core, 1 - core):
+            if step == 0 and c is core:
+                continue
+            row = ask_v.at[pl.ds(mine, 1)]
+            send(row, row, ask_send.at[0], ask_recv.at[0], moved(me, "y", step), c)
+
+    def spread(parts):
+        for k in parts:
+            order, r0, c0, cols = PARTS[k]
+            axis = ORDERS[order][0]
+            src = mult_ref.at[:, pl.ds(r0, ROWS), pl.ds(c0, cols)]
+            dst = gathered[k].at[pl.ds(me[axis] * 32, 32)]
+            pltpu.make_async_copy(src, dst, g_own.at[k]).start()
+            for step in (1, 3, 2):
+                send(src, dst, g_send.at[k], g_recv.at[k], moved(me, axis, step), core)
+
+    drain(ask_v.at[pl.ds(0, 7)], ask_recv.at[0])
+    for step in (1, 3, 2):
+        part = ask_v.at[pl.ds(slab * 8, 8)]
+        send(part, part, ask_send.at[1], ask_recv.at[1], moved(me, "z", step), core)
+    spread((0, 1, 2))
+    drain(ask_v.at[pl.ds(0, 24)], ask_recv.at[1])
+    for step in (1, 3, 2):
+        part = ask_v.at[pl.ds(me["x"] * 32, 32)]
+        send(part, part, ask_send.at[2], ask_recv.at[2], moved(me, "x", step), core)
+    spread((3, 4, 5))
+    drain(ask_v.at[pl.ds(0, 96)], ask_recv.at[2])
+    to_scalars = pltpu.make_async_copy(ask_v, ask_s, copy_sem)
+    to_scalars.start()
+    to_scalars.wait()
+
+    def pack(k):
+        order, r0, c0, cols = PARTS[k]
+        g, p, q = ORDERS[order]
+        drain(gathered[k].at[pl.ds(0, 96)], g_recv.at[k])
+        drain(gathered[k].at[pl.ds(0, 32)], g_own.at[k])
+        for step in (1, 3, 2, 0):
+            target = moved(me, p, step)
+
+            def one(j, _):
+                to = dict(target)
+                to[q] = j // 8
+                asker = index_of(to, (j // 4) % 2)
+                source = dict(me)
+                source[g] = j % 4
+                served = index_of(source, core)
+                for r in range(2):
+                    row = ask_s[asker, r, served]
+                    packed[k][target[p], 2 * j + r] = gathered[k][(j % 4) * 32 + row]
+                return 0
+
+            lax.fori_loop(0, 32, one, 0, unroll=4)
+            if step:
+                send(packed[k].at[target[p]], relay[k].at[me[p]], s_send.at[k], s_recv.at[k, me[p]], target, core)
+
+    def forward(k, step):
+        order = PARTS[k][0]
+        g, p, q = ORDERS[order]
+        came = moved(me, p, step)
+        src = packed[k] if step == 0 else relay[k]
+        if step:
+            drain(relay[k].at[came[p]], s_recv.at[k, came[p]])
+        slot = ((came[p] * 4 + me[q]) * 2 + core) * 8
+        for hop in (1, 3, 2, 0):
+            for c in (core, 1 - core):
+                to = moved(me, q, hop)
+                piece = src.at[came[p], pl.ds((to[q] * 2 + c) * 8, 8)]
+                dst = finals[k].at[pl.ds(slot, 8)]
+                if hop == 0 and c is core:
+                    pltpu.make_async_copy(piece, dst, f_own.at[k]).start()
+                else:
+                    send(piece, dst, f_send.at[k], f_recv.at[k], to, c)
+
+    for k in range(6):
+        pack(k)
+        forward(k, 0)
+    for k in range(6):
+        for step in (1, 3, 2):
+            forward(k, step)
+
+    for k in range(6):
+        drain(finals[k].at[pl.ds(0, 224)], f_recv.at[k])
+        drain(finals[k].at[pl.ds(0, 32)], f_own.at[k])
+        drain(finals[k].at[pl.ds(0, 224)], f_send.at[k])
+        drain(packed[k].at[pl.ds(0, 3)], s_send.at[k])
+        drain(gathered[k].at[pl.ds(0, 96)], g_send.at[k])
+    drain(ask_v.at[pl.ds(0, 7)], ask_send.at[0])
+    drain(ask_v.at[pl.ds(0, 24)], ask_send.at[1])
+    drain(ask_v.at[pl.ds(0, 96)], ask_send.at[2])
+
+
+def exchange(owner, box, multipoles):
+    any_space = pl.BlockSpec(memory_space=pl.ANY)
+    vmem = pl.BlockSpec(memory_space=pltpu.VMEM)
+    dma = pltpu.SemaphoreType.DMA
+    return pl.pallas_call(
+        exchange_kernel,
+        out_shape=[jax.ShapeDtypeStruct((256, ROWS, part[3]), jnp.bfloat16) for part in PARTS],
+        in_specs=[vmem, vmem, any_space],
+        out_specs=[any_space] * 6,
+        scratch_shapes=[pltpu.VMEM((128, ROWS, part[3]), jnp.bfloat16) for part in PARTS]
+        + [pltpu.VMEM((4, 64, ROWS, part[3]), jnp.bfloat16) for part in PARTS]
+        + [pltpu.VMEM((4, 64, ROWS, part[3]), jnp.bfloat16) for part in PARTS]
+        + [
+            pltpu.VMEM((128, 2, 128), jnp.int32),
+            pltpu.SMEM((128, 2, 128), jnp.int32),
+            dma((3,)), dma((3,)), dma, dma((6,)), dma((6,)), dma((6,)), dma((6,)), dma((6, 4)), dma((6,)), dma((6,)), dma((6,)),
+        ],
+        compiler_params=pltpu.CompilerParams(collective_id=0, has_side_effects=True, vmem_limit_bytes=60 * 2**20),
+    )(owner, box, multipoles)
 
 
 def extended(cells, sides, width):
@@ -27,6 +199,26 @@
     return cells
 
 
+length_factor = 1.7320508075688772
+
+
+def extended(cells, sides, width):
+    for axis, dim in sides:
+        count = lax.axis_size(axis)
+        ends = count - 1
+        head = lax.slice_in_dim(cells, 0, width, axis=dim)
+        tail = lax.slice_in_dim(cells, cells.shape[dim] - width, cells.shape[dim], axis=dim)
+        cells = jnp.concatenate(
+            [
+                lax.ppermute(tail, axis, [(i, (i + 1) % count) for i in range(ends)]),
+                cells,
+                lax.ppermute(head, axis, [((i + 1) % count, i) for i in range(ends)]),
+            ],
+            axis=dim,
+        )
+    return cells
+
+
 def node_weights(coord):
     steps = jnp.arange(ORDER).astype(jnp.float32)
     angles = (2.0 * steps + 1.0) * jnp.pi / (2.0 * ORDER)
@@ -61,27 +253,22 @@
     multipoles, translations, local_source, remote_owner, remote_box, charges, positions, leaf_count
 ):
     boxes, rhs, coefs = multipoles.shape
-    devices = lax.axis_size(("slab", "sub"))
     local_types = local_source.shape[0]
-    remote_rows = remote_box.shape[0]
-    remote_types = remote_rows // boxes
-    capacity = max(2, (remote_rows + devices - 1) // devices)
-    local_blocks = jnp.take(multipoles, local_source.reshape(-1), axis=0).reshape(
+    remote_types = remote_box.shape[0] // boxes
+    local_blocks = jnp.take(multipoles, local_source.reshape(-1), axis=0, mode="clip").reshape(
         local_types, boxes, rhs, coefs
     )
+    arrived = exchange(remote_owner, remote_box[:, None], multipoles)
     owner = remote_owner[:, 0]
-    onehot = (owner[:, None] == jnp.arange(devices)[None, :]).astype(jnp.int32)
-    before = jnp.cumsum(onehot, axis=0) - onehot
-    rank = jnp.sum(before * onehot, axis=1)
-    slot_index = owner * capacity + rank
-    wanted = jnp.zeros((devices * capacity,), jnp.int32).at[slot_index].set(remote_box)
-    asked = lax.all_to_all(
-        wanted.reshape(devices, capacity), ("slab", "sub"), split_axis=0, concat_axis=0, tiled=True
-    )
-    served = jnp.take(multipoles, asked.reshape(-1), axis=0).reshape(devices, capacity, rhs, coefs)
-    arrived = lax.all_to_all(served, ("slab", "sub"), split_axis=0, concat_axis=0, tiled=True)
-    arrived = arrived.reshape(devices * capacity, rhs, coefs)
-    remote_blocks = jnp.take(arrived, slot_index, axis=0).reshape(remote_types, boxes, rhs, coefs)
+    rank = jnp.sum(jnp.tril(owner[:, None] == owner[None, :], -1).astype(jnp.int32), axis=1)
+    pieces = []
+    for (order, _, _, _), part in zip(PARTS, arrived):
+        at = {"x": owner // 32, "z": owner // 8 % 4, "y": owner // 2 % 4}
+        g, p, q = (at[axis] for axis in ORDERS[order])
+        slot = ((p * 4 + q) * 2 + owner % 2) * 8 + g * 2 + rank
+        pieces.append(jnp.take(part, slot, axis=0, mode="clip"))
+    last = jnp.concatenate(pieces[3:], 2)
+    remote_blocks = jnp.concatenate(pieces[:3] + [last], 1).reshape(remote_types, boxes, rhs, coefs)
     sources = jnp.concatenate([local_blocks, remote_blocks], 0)
     expansion = jnp.einsum(
         "tbrp,tpq->brq", sources, translations, preferred_element_type=jnp.float32

time: 378 us -> 318 us (0.84)
  the two profiles are of different devices: /device:TPU:98 before, /device:TPU:1 now
where the time goes in v1:
time: 318 us; the launch traced here: 315 us
  Pallas kernels  172 us (54%)
  matrix products  55 us (17%)
  local copies, waits for them, and re-layouts  52.1 us (16%)
  other arithmetic  27.9 us (9%)
  starting transfers between devices  6.52 us (2%)
    pallas_call x1, Pallas kernels, exchange(): pl.pallas_call(exchange_kernel, out_shape=[jax.ShapeDtypeStruct((256, ROW...  172 us
    dot_general x1, matrix products, on_device(): jnp.einsum('tbrp,tpq->brq', sources, translations, preferred_element_type...  35.8 us
    gather x6, local copies, waits for them, and re-layouts, on_device(): pieces.append(jnp.take(part, slot, axis=0, mode='clip'))  22.3 us
    gather x1, local copies, waits for them, and re-layouts, on_device(): jnp.take(multipoles, local_source.reshape(-1), axis=0, mode='clip')  16.1 us
    dot_general x1, matrix products, on_device(): jnp.einsum('brp,bqp->rbq', expansion, weights, precision=lax.Precision.HI...  13 us
    concatenate x1, other arithmetic, on_device(): jnp.concatenate(pieces[:3] + [last], 1)  11.4 us
    sub x1, other arithmetic, near_field(): diff = targets[:, :, :, None, None] - source_pos[:, :, None, :, :]  10.3 us
    mul x1, local copies, waits for them, and re-layouts, interpolate(): first[:, :, None, None] * second[:, None, :, None] * third[:, None, None, :]  7.83 us
  transfers between devices with their start and end apart: 2, of which 0 were waited for; matrix products, arithmetic and copies ran while one was open for 32% of the time, Pallas kernels for 55%

profile of v1, /device:TPU:1, one launch (start us, length us, event | category | flops | bytes accessed | tf_op | source)
XLA Modules:
  0.0 315.2 jit_solution(9196092572022680466)
XLA Ops:
  0.7 0.7 fusion.51
  1.4 1.4 reshape.244
  2.8 0.9 reshape.239
  3.7 0.6 copy_multiply_fusion
  4.3 4.6 %collective-permute-start = (f32[67,1,64]{2,0,1:T(8,128)S(1)}, f32[67,1,64]{2,0,1:T(8,128)S(1)}, u32[]{:S(2)}, u32[]{:S(2)}) collective-permute-start(f32[67,1,64]{2,0,1:T(8,128)S(1)} %get-tuple-element.25), channel_id=1, source_target_pairs={{0,1},{1,2},{2,3},{3,4},{4,5},{5,6},{6,7},{7,8},{8,9},{9,10},{10,1... | collective-permute-start | bytes 51464 | tf_op jit(solution)/shard_map/ppermute | solution.py:213
  8.9 1.9 collective-permute-start.1
  10.9 0.8 copy.29.owner_ref
  11.7 0.2 convert_reduce_fusion
  12.0 0.8 copy.30.box_ref
  12.8 172.5 %shard_map.95 = (bf16[256,16,512]{2,1,0:T(8,128)(2,1)}, bf16[256,16,512]{2,1,0:T(8,128)(2,1)}, bf16[256,16,512]{2,1,0:T(8,128)(2,1)}, bf16[256,16,128]{2,1,0:T(8...) custom-call(s32[256,1]{1,0:T(8,128)} %copy.29.owner_ref, s32[256,1]{1,0:T(8,128)} %copy.30.box_ref, ...), custom_call_target="tpu_custom_call" | custom-call | tf_op jit(solution)/shard_map/pallas_call | solution.py:168
  185.3 5.2 %gather_fusion.3 = bf16[256,16,512]{2,1,0:T(8,128)(2,1)} fusion(bf16[256,16,512]{2,1,0:T(8,128)(2,1)} %get-tuple-element.10, s32[1024]{0:T(1024)S(1)} %pad_clamp_fusion), kind=kCustom, calls=%fused_computation.3 | custom fusion | bytes 8389632 | tf_op jit(solution)/shard_map/jit(_take)/gather | solution.py:269
  190.5 2.1 gather_fusion.6
  192.6 5.2 %gather_fusion.2 = bf16[256,16,512]{2,1,0:T(8,128)(2,1)} fusion(bf16[256,16,512]{2,1,0:T(8,128)(2,1)} %get-tuple-element.9, s32[1024]{0:T(1024)S(1)} %pad_clamp_fusion.1), kind=kCustom, calls=%fused_computation.2 | custom fusion | bytes 8389632 | tf_op jit(solution)/shard_map/jit(_take)/gather | solution.py:269
  197.7 1.8 gather_fusion.5
  199.5 5.1 %gather_fusion.1 = bf16[256,16,512]{2,1,0:T(8,128)(2,1)} fusion(bf16[256,16,512]{2,1,0:T(8,128)(2,1)} %get-tuple-element.8, s32[1024]{0:T(1024)S(1)} %pad_clamp_fusion.2), kind=kCustom, calls=%fused_computation.1 | custom fusion | bytes 8389632 | tf_op jit(solution)/shard_map/jit(_take)/gather | solution.py:269
  204.7 3.0 gather_fusion.4
  207.7 0.1 reshape.247
  207.8 16.1 %gather_fusion = bf16[512,64,512]{2,1,0:T(8,128)(2,1)} fusion(bf16[32,64,512]{2,1,0:T(8,128)(2,1)S(1)} %copy-done, s32[1024]{0:T(1024)S(1)} %pad_clamp_fusion.3), kind=kCustom, calls=%fused_computation | custom fusion | bytes 67110912 | tf_op jit(solution)/shard_map/jit(_take)/gather | solution.py:258
  224.0 0.1 multiply_cosine_fusion.3
  224.1 0.7 multiply_cosine_fusion
  224.8 0.5 multiply_reduce_fusion.2
  225.4 2.5 broadcast_multiply_fusion
  227.9 11.4 %maximum_maximum_fusion = bf16[256,64,512]{2,1,0:T(8,128)(2,1)} fusion(bf16[256,16,256]{2,1,0:T(8,128)(2,1)S(1)} %copy-done.2, bf16[256,16,128]{2,1,0:T(8,128)(2,1)} %gather_fusion.5, bf16[256,16,128]{2,1,0:T(8,128)(2,1)} %gather_fusion.4, bf16[256,16,512]{2,1,0:T(8,128)(2,1)S(1)} %copy-done.1, bf16[256,16,512]{2,1,0:T(8,128)(2,1)} %gather_fusion.2, ...), kind=kLoop, calls=%fused_computation.11 | loop fusion | flops 100663296 | bytes 33554432 | tf_op jit(solution)/shard_map/concatenate | solution.py:271
  239.3 35.8 %fusion.22 = f32[32,64,512]{2,1,0:T(8,128)} fusion(bf16[24,512,512]{2,1,0:T(8,128)(2,1)} %param.9, bf16[8,32,64,512]{3,2,1,0:T(8,128)(2,1)} %bitcast.89, bf16[16,32,64,512]{3,2,1,0:T(8,128)(2,1)} %bitcast.86), kind=kOutput, calls=%fused_computation.34 | convolution fusion | flops 25794969600 | bytes 67108864 | tf_op jit(solution)/shard_map/tbrp,tpq->brq/dot_general | solution.py:273
  275.2 7.8 %mul.369 = f32[32,64,512]{1,0,2:T(8,128)} reshape(f32[2048,8,8,8]{0,3,2,1:T(8,128)} %broadcast_multiply_fusion) | data formatting | bytes 8388608 | tf_op jit(solution)/shard_map/mul | solution.py:236
  283.0 0.2 fusion.47
  283.3 0.2 pad_maximum_fusion
  283.6 10.3 %broadcast_subtract_fusion = f32[3,32,64,3,64]{4,2,3,1,0:T(8,128)S(1)} fusion(f32[3,32,3,64]{3,2,1,0:T(4,128)S(1)} %copy.37, f32[3,32,64]{2,1,0:T(8,128)S(1)} %reshape.239), kind=kLoop, calls=%fused_computation.15 | loop fusion | flops 1179648 | bytes 4816896 | tf_op jit(solution)/shard_map/sub | solution.py:244
  294.0 6.2 %fusion.40 = f32[64,32,64]{2,0,1:T(8,128)S(1)} fusion(f32[3,32,64,3,64]{4,2,3,1,0:T(8,128)S(1)} %broadcast_subtract_fusion, f32[3]{0:T(128)S(1)} %add_multiply_fusion.4, f32[67,3,32,64]{3,0,1,2:T(8,128)S(1)} %pad_maximum_fusion), kind=kOutput, calls=%fused_computation.46 | convolution fusion | flops 305922048 | bytes 13107712 | tf_op jit(solution)/shard_map/lqos,rols->rlq/dot_general | solution.py:249
  300.2 13.0 %fusion.37 = f32[64,32,64]{2,0,1:T(8,128)S(1)} fusion(f32[64,32,64]{2,0,1:T(8,128)S(1)} %fusion.40, f32[32,64,512]{2,1,0:T(8,128)S(1)} %copy-done.3, f32[32,64,512]{1,0,2:T(8,128)S(1)} %bitcast.88, f32[32,64]{1,0:T(8,128)S(1)} %fusion.51), kind=kOutput, calls=%fused_computation.45 | convolution fusion | flops 805568512 | bytes 9445376 | tf_op jit(solution)/shard_map/brp,bqp->rbq/dot_general | solution.py:278
  313.2 0.6 copy.40
  313.8 1.2 reshape.242
  (48 shorter events, 0.5 us)
Async XLA Ops:
  0.6 10.2 %copy-start.6 = (f32[3,2048]{1,0:T(4,128)S(1)}, f32[3,2048]{1,0:T(4,128)}, u32[]{:S(2)}) copy-start(f32[3,2048]{1,0:T(4,128)} %param.14) | copy-start | bytes 73732
  0.6 10.3 %copy-start.7 = (s32[256,1]{0,1:T(1,128)S(1)}, s32[256,1]{0,1:T(1,128)}, u32[]{:S(2)}) copy-start(s32[256,1]{0,1:T(1,128)} %param.11) | copy-start | bytes 3076
  0.7 11.4 %copy-start.9 = (s32[256]{0:T(256)S(1)}, s32[256]{0:T(256)}, u32[]{:S(2)}) copy-start(s32[256]{0:T(256)} %param.12) | copy-start | bytes 3076
  4.3 278.7 %collective-permute-start = (f32[67,1,64]{2,0,1:T(8,128)S(1)}, f32[67,1,64]{2,0,1:T(8,128)S(1)}, u32[]{:S(2)}, u32[]{:S(2)}) collective-permute-start(f32[67,1,64]{2,0,1:T(8,128)S(1)} %get-tuple-element.25), channel_id=1, source_target_pairs={{0,1},{1,2},{2,3},{3,4},{4,5},{5,6},{6,7},{7,8},{8,9},{9,10},{10,1... | collective-permute-start | bytes 51464 | tf_op jit(solution)/shard_map/ppermute | solution.py:213
  8.9 274.1 %collective-permute-start.1 = (f32[67,1,64]{2,0,1:T(8,128)S(1)}, f32[67,1,64]{2,0,1:T(8,128)S(1)}, u32[]{:S(2)}, u32[]{:S(2)}) collective-permute-start(f32[67,1,64]{2,0,1:T(8,128)S(1)} %get-tuple-element.26), channel_id=1, source_target_pairs={{1,0},{2,1},{3,2},{4,3},{5,4},{6,5},{7,6},{8,7},{9,8},{10,9},{11,1... | collective-permute-start | bytes 51464 | tf_op jit(solution)/shard_map/ppermute | solution.py:215
  185.3 5.2 %copy-start.4 = (bf16[256,16,256]{2,1,0:T(8,128)(2,1)S(1)}, bf16[256,16,256]{2,1,0:T(8,128)(2,1)}, u32[]{:S(2)}) copy-start(bf16[256,16,256]{2,1,0:T(8,128)(2,1)} %get-tuple-element.13) | copy-start | bytes 6291460
  192.6 5.2 %copy-start.5 = (bf16[256,16,128]{2,1,0:T(8,128)(2,1)S(1)}, bf16[256,16,128]{2,1,0:T(8,128)(2,1)}, u32[]{:S(2)}) copy-start(bf16[256,16,128]{2,1,0:T(8,128)(2,1)} %get-tuple-element.12) | copy-start | bytes 3145732
  199.5 8.2 %copy-start.8 = (s32[16,32]{1,0:T(8,128)S(1)}, s32[16,32]{1,0:T(8,128)}, u32[]{:S(2)}) copy-start(s32[16,32]{1,0:T(8,128)} %param.10) | copy-start | bytes 6148
  199.5 8.2 %copy-start = (bf16[32,64,512]{2,1,0:T(8,128)(2,1)S(1)}, bf16[32,64,512]{2,1,0:T(8,128)(2,1)}, u32[]{:S(2)}) copy-start(bf16[32,64,512]{2,1,0:T(8,128)(2,1)} %mult_ref.1) | copy-start | bytes 6291460
  223.9 4.0 %copy-start.1 = (bf16[256,16,512]{2,1,0:T(8,128)(2,1)S(1)}, bf16[256,16,512]{2,1,0:T(8,128)(2,1)}, u32[]{:S(2)}) copy-start(bf16[256,16,512]{2,1,0:T(8,128)(2,1)} %gather_fusion.3) | copy-start | bytes 12582916
  223.9 4.0 %copy-start.2 = (bf16[256,16,256]{2,1,0:T(8,128)(2,1)S(1)}, bf16[256,16,256]{2,1,0:T(8,128)(2,1)}, u32[]{:S(2)}) copy-start(bf16[256,16,256]{2,1,0:T(8,128)(2,1)} %gather_fusion.6) | copy-start | bytes 6291460
  283.6 16.6 %slice-start = ((s8[8388608]{0:T(1024)(128)(4,1)}), s8[4194304]{0:T(1024)(128)(4,1)S(1)}, s32[]{:S(2)}) async-start(s8[8388608]{0:T(1024)(128)(4,1)} %bitcast.87), calls=%async_computation | async-start | bytes 8388608
  293.9 6.3 %slice-start.1 = ((s8[8388608]{0:T(1024)(128)(4,1)}), s8[4194304]{0:T(1024)(128)(4,1)S(1)}, s32[]{:S(2)}) async-start(s8[8388608]{0:T(1024)(128)(4,1)} %bitcast.87), calls=%async_computation.1 | async-start | bytes 8388608
  293.9 6.3 %copy-start.3 = (f32[32,64,512]{2,1,0:T(8,128)S(1)}, f32[32,64,512]{2,1,0:T(8,128)}, u32[]{:S(2)}) copy-start(f32[32,64,512]{2,1,0:T(8,128)} %fusion.22) | copy-start | bytes 12582916

commit v2 on v1

v2 whole, which is shorter than its diff:
```python
import math

import jax
import jax.numpy as jnp
from jax import lax
from jax.experimental import pallas as pl
from jax.experimental.pallas import tpu as pltpu
from jax.sharding import PartitionSpec as P

ORDER = 8
SLOTS = 64
length_factor = 1.7320508075688772
MESH = pl.DeviceIdType.MESH

PARTS = ((0, 0, 0, 512), (1, 16, 0, 512), (2, 32, 0, 512), (0, 48, 0, 128), (1, 48, 128, 128), (2, 48, 256, 256))
ORDERS = ("xyz", "yzx", "zxy")
ROWS = 16


def place(at, core):
    return (at["x"] * 4 + at["z"], at["y"] * 2 + core)


def index_of(at, core):
    return at["x"] * 32 + at["z"] * 8 + at["y"] * 2 + core


def moved(at, axis, step):
    other = dict(at)
    other[axis] = (at[axis] + step) % 4
    return other


def dot(a, b):
    return jnp.dot(a, b, preferred_element_type=jnp.float32)


def split(value):
    high = value.astype(jnp.bfloat16)
    return high, (value - high.astype(jnp.float32)).astype(jnp.bfloat16)


def whole_kernel(
    owner_ref, box_ref, local_ref, count_ref, mult_ref, ops_ref, charge_ref, pos_ref, expansion_ref, potential_ref, *scratch
):
    relay, scratch = scratch[0:6], scratch[6:]
    gathered, packed, finals = scratch[0:6], scratch[6:12], scratch[12:18]
    ask_v, ask_s, slot_v, slot_s = scratch[18:22]
    mult, ops, stream, total, lhs, charges, places, shifted, columns, tables, edge_out, edge_in = scratch[22:34]
    (ask_send, ask_recv, copy_sem, g_send, g_recv, g_own, s_send, s_recv, f_send, f_recv, f_own) = scratch[34:45]
    load_sem, stream_sem, edge_send, edge_recv, out_sem = scratch[45:]
    loads = [
        pltpu.make_async_copy(charge_ref, charges, load_sem.at[0]),
        pltpu.make_async_copy(pos_ref, places.at[pl.ds(0, 3)], load_sem.at[1]),
        pltpu.make_async_copy(mult_ref, mult, load_sem.at[2]),
        pltpu.make_async_copy(ops_ref.at[pl.ds(16, 8)], ops, load_sem.at[3]),
    ]
    places[...] = jnp.zeros_like(places)
    for load in loads:
        load.start()
    slab, sub = lax.axis_index("slab"), lax.axis_index("sub")
    me = {"x": slab // 4, "y": sub // 2, "z": slab % 4}
    core = sub % 2
    mine = index_of(me, core)

    barrier = pltpu.get_barrier_semaphore()
    partners = [(me, 1 - core)]
    for axis in "xyz":
        for step in (1, 3, 2):
            for other in (core, 1 - core):
                partners.append((moved(me, axis, step), other))
    for z in (1, 3, 2):
        for x in (1, 3, 2):
            partners.append((moved(moved(me, "z", z), "x", x), core))
    for at, c in partners:
        pl.semaphore_signal(barrier, 1, device_id=place(at, c), device_id_type=MESH)
    after, prior = (mine + 1) % 128, (mine + 127) % 128
    for number in (after, prior):
        pl.semaphore_signal(barrier, 1, device_id=(number // 8, number % 8), device_id_type=MESH)

    owner, box = owner_ref[...], box_ref[...]
    rows = owner.shape[0]
    down = lax.broadcasted_iota(jnp.int32, (rows, rows), 0)
    along = lax.broadcasted_iota(jnp.int32, (rows, rows), 1)
    across = jnp.sum(jnp.where(down == along, owner, 0), axis=0, keepdims=True)
    before = jnp.where((owner == across) & (along < down), 1, 0)
    rank = jnp.sum(before, axis=1, keepdims=True)
    row_rank = jnp.sum(jnp.where((owner == across) & (down < along), 1, 0), axis=0, keepdims=True)
    spots = {"x": across // 32, "z": across // 8 % 4, "y": across // 2 % 4}
    for order in range(3):
        g, p, q = (spots[axis] for axis in ORDERS[order])
        slot_v[order : order + 1, :] = ((p * 4 + q) * 2 + across % 2) * 8 + g * 2 + row_rank
    slot_v[3:8, :] = jnp.zeros((5, rows), jnp.int32)
    to_slots = pltpu.make_async_copy(slot_v, slot_s, copy_sem.at[1])
    to_slots.start()
    named = owner == lax.broadcasted_iota(jnp.int32, (rows, 128), 1)
    for r in range(2):
        wanted = jnp.sum(jnp.where(named & (rank == r), box, 0), axis=0, keepdims=True)
        ask_v[mine, r : r + 1, :] = wanted

    pl.semaphore_wait(barrier, len(partners) + 2)

    def send(src, dst, ssem, rsem, at, c):
        pltpu.make_async_remote_copy(
            src_ref=src, dst_ref=dst, send_sem=ssem, recv_sem=rsem, device_id=place(at, c), device_id_type=MESH
        ).start()

    def drain(ref, sem):
        pltpu.make_async_copy(ref, ref, sem).wait()

    lane = lax.broadcasted_iota(jnp.int32, (1, 128), 1)
    second = lane >= 64

    def tile(i):
        return pl.ds(pl.multiple_of(i * 128, 128), 128)

    def present(i):
        return (lane % 64) < jnp.where(second, count_ref[2 * i + 1], count_ref[2 * i])

    def masked(i):
        return jnp.where(present(i), charges[:, tile(i)].astype(jnp.float32), 0.0)

    def send_edges():
        loads[0].wait()
        loads[1].wait()
        for way, (i, number) in enumerate(((15, after), (0, prior))):
            edge_out[way, 0:64, :] = masked(i)
            edge_out[way, 64:72, :] = places[:, tile(i)]
            pltpu.make_async_remote_copy(
                src_ref=edge_out.at[way],
                dst_ref=edge_in.at[way],
                send_sem=edge_send.at[way],
                recv_sem=edge_recv.at[way],
                device_id=(number // 8, number % 8),
                device_id_type=MESH,
            ).start()

    for step in (0, 1, 3, 2):
        for c in (core, 1 - core):
            if step == 0 and c is core:
                continue
            row = ask_v.at[pl.ds(mine, 1)]
            send(row, row, ask_send.at[0], ask_recv.at[0], moved(me, "y", step), c)

    drain(ask_v.at[pl.ds(0, 7)], ask_recv.at[0])
    send_edges()
    for step in (1, 3, 2):
        part = ask_v.at[pl.ds(slab * 8, 8)]
        send(part, part, ask_send.at[1], ask_recv.at[1], moved(me, "z", step), core)
        send(part, part, ask_send.at[1], ask_recv.at[1], moved(me, "x", step), core)
    for z in (1, 3, 2):
        for x in (1, 3, 2):
            part = ask_v.at[pl.ds(slab * 8 + me["y"] * 2, 2)]
            send(part, part, ask_send.at[1], ask_recv.at[1], moved(moved(me, "z", z), "x", x), core)

    def boxes_of(k, at, first, count):
        return gathered[k].at[pl.ds(at[ORDERS[PARTS[k][0]][0]] * 32 + first, count)]

    for k, (order, r0, c0, cols) in enumerate(PARTS):
        axis = ORDERS[order][0]
        src = mult_ref.at[:, pl.ds(r0, ROWS), pl.ds(c0, cols)]
        dst = boxes_of(k, me, 0, 32)
        send(src, dst, g_send.at[k], g_recv.at[k, 0], moved(me, axis, 1), core)
        send(src, dst, g_send.at[k], g_recv.at[k, 1], moved(me, axis, 3), core)
        pltpu.make_async_copy(src, dst, g_own.at[k]).start()
    drain(ask_v.at[pl.ds(0, 66)], ask_recv.at[1])
    to_scalars = pltpu.make_async_copy(ask_v, ask_s, copy_sem.at[0])
    to_scalars.start()
    for k in range(6):
        axis = ORDERS[PARTS[k][0]][0]
        for way, step in ((0, 3), (1, 1)):
            came = moved(me, axis, step)
            drain(boxes_of(k, came, 0, 32), g_recv.at[k, way])
            half = boxes_of(k, came, 16 * way, 16)
            send(half, half, g_send.at[k], g_recv.at[k, 2], moved(me, axis, 4 - step), core)
    to_scalars.wait()

    def pack(k):
        order, r0, c0, cols = PARTS[k]
        g, p, q = ORDERS[order]
        drain(gathered[k].at[pl.ds(0, 32)], g_recv.at[k, 2])
        drain(gathered[k].at[pl.ds(0, 32)], g_own.at[k])
        for step in (1, 3, 2, 0):
            target = moved(me, p, step)

            def one(j, _):
                to = dict(target)
                to[q] = j // 8
                asker = index_of(to, (j // 4) % 2)
                source = dict(me)
                source[g] = j % 4
                served = index_of(source, core)
                for r in range(2):
                    row = ask_s[asker, r, served]
                    packed[k][target[p], 2 * j + r] = gathered[k][(j % 4) * 32 + row]
                return 0

            lax.fori_loop(0, 32, one, 0, unroll=4)
            if step:
                send(packed[k].at[target[p]], relay[k].at[me[p]], s_send.at[k], s_recv.at[k, me[p]], target, core)

    def forward(k, step):
        order = PARTS[k][0]
        g, p, q = ORDERS[order]
        came = moved(me, p, step)
        src = packed[k] if step == 0 else relay[k]
        if step:
            drain(relay[k].at[came[p]], s_recv.at[k, came[p]])
        slot = ((came[p] * 4 + me[q]) * 2 + core) * 8
        for hop in (1, 3, 2, 0):
            for c in (core, 1 - core):
                to = moved(me, q, hop)
                piece = src.at[came[p], pl.ds((to[q] * 2 + c) * 8, 8)]
                dst = finals[k].at[pl.ds(slot, 8)]
                if hop == 0 and c is core:
                    pltpu.make_async_copy(piece, dst, f_own.at[k]).start()
                else:
                    send(piece, dst, f_send.at[k], f_recv.at[k], to, c)

    def near_sums():
        for way in range(2):
            drain(edge_in.at[way], edge_recv.at[way])
            drain(edge_out.at[way], edge_send.at[way])
        here = (mine > 0, mine < 127)
        for way in range(2):
            edge_in[way, 0:64, :] = jnp.where(here[way], edge_in[way, 0:64, :], 0.0)

        def half(i, before, now):
            joined = jnp.where(second, pltpu.roll(now, 64, 1), pltpu.roll(before, 64, 1))
            shifted[:, tile(i)] = joined[0:64].astype(jnp.bfloat16)
            columns[tile(i), 0:8] = jnp.transpose(joined[64:72])

        def own(i):
            return jnp.concatenate([masked(i), places[:, tile(i)]], 0)

        half(0, edge_in[0], own(0))
        half(16, own(15), edge_in[1])

        def middle(i, _):
            half(i, own(i - 1), own(i))
            return 0

        lax.fori_loop(1, 16, middle, 0)

        def pair(i, _):
            kernel_tiles = []
            for sb in range(4):
                o = jnp.where(second, sb - 2, sb - 1)
                at = columns[pl.ds(pl.multiple_of(i * 128 + sb * 64, 64), 64), 0:8]
                dx = places[0:1, tile(i)] - at[:, 0:1] - 2.0 * o.astype(jnp.float32)
                dy = places[1:2, tile(i)] - at[:, 1:2]
                dz = places[2:3, tile(i)] - at[:, 2:3]
                scaled = length_factor * jnp.sqrt(dx * dx + dy * dy + dz * dz)
                value = (1.0 + scaled) * jnp.exp(-scaled)
                kernel_tiles.append(jnp.where((o >= -1) & (o <= 1), value, 0.0))
            high, low = split(jnp.concatenate(kernel_tiles, 0))
            window = shifted[:, pl.ds(pl.multiple_of(i * 128, 128), 256)]
            potential_ref[:, tile(i)] = dot(window, high) + dot(window, low)
            return 0

        lax.fori_loop(0, 16, pair, 0)

    def weight_tables():
        node = lax.broadcasted_iota(jnp.int32, (8, 128), 0)
        factors = []
        for k in range(ORDER):
            column = jnp.zeros((8, 128), jnp.float32)
            for m in range(ORDER):
                column = jnp.where(node == m, math.cos(k * (2 * m + 1) * math.pi / (2 * ORDER)), column)
            factors.append(column)

        def pair(i, _):
            weights = []
            for axis in range(3):
                u = places[axis : axis + 1, tile(i)]
                old, new = jnp.ones_like(u), u
                value = factors[0] + factors[1] * u
                for k in range(2, ORDER):
                    old, new = new, 2.0 * u * new - old
                    value = value + factors[k] * new
                weights.append((2.0 * value - 1.0) / ORDER)
            for m1 in range(ORDER):
                parts = [(weights[0][m1 : m1 + 1] * weights[1][m2 : m2 + 1]) * weights[2] for m2 in range(ORDER)]
                high, low = split(jnp.concatenate(parts, 0))
                tables[i, m1 * 64 : m1 * 64 + 64, 0:128] = high
                tables[i, m1 * 64 : m1 * 64 + 64, 128:256] = low
            return 0

        lax.fori_loop(0, 16, pair, 0)

    def load_op(t):
        return pltpu.make_async_copy(ops_ref.at[t], stream.at[t % 2], stream_sem.at[t % 2])

    def local_type(t):
        load_op(t).wait()
        if t + 1 < 16:
            load_op(t + 1).start()

        def group(i, _):
            for b in range(8):
                lhs[b * 64 : b * 64 + 64, :] = mult[local_ref[t, i * 8 + b]]
            value = dot(lhs[...], stream[t % 2]).reshape(8, 64, 512)
            if t == 0:
                total[pl.ds(i * 8, 8)] = value
            else:
                total[pl.ds(i * 8, 8)] += value
            return 0

        lax.fori_loop(0, 4, group, 0)

    def remote_rows(parts):
        r0 = PARTS[parts[0]][1]
        for k in parts:
            drain(finals[k].at[pl.ds(0, 224)], f_recv.at[k])
            drain(finals[k].at[pl.ds(0, 32)], f_own.at[k])

        def one(t, _):
            at = 0
            for k in parts:
                order, _, c0, cols = PARTS[k]
                for b in range(32):
                    lhs[b * 16 : b * 16 + 16, c0 : c0 + cols] = finals[k][slot_s[order, t * 32 + b]]
            total[:, r0 : r0 + ROWS, :] += dot(lhs[...], ops[t]).reshape(32, ROWS, 512)
            return 0

        lax.fori_loop(0, 8, one, 0)

    def store_rows(r0, count):
        return pltpu.make_async_copy(
            total.at[:, pl.ds(r0, count)], expansion_ref.at[:, pl.ds(r0, count)], out_sem.at[r0 // 48]
        )

    def far_rows(r0, count):
        def pair(i, _):
            value = total[pl.ds(2 * i, 2), r0 : r0 + count, :].reshape(2 * count, 512)
            high, low = split(value)
            both = dot(jnp.concatenate([high, low], 0), tables[i])
            summed = both[: 2 * count, 0:128] + both[: 2 * count, 128:256] + both[2 * count :, 0:128]
            far = jnp.where(second, summed[count:], summed[:count])
            near = potential_ref[r0 : r0 + count, tile(i)]
            potential_ref[r0 : r0 + count, tile(i)] = jnp.where(present(i), near + far, 0.0)
            return 0

        lax.fori_loop(0, 16, pair, 0)

    load_op(0).start()
    for k in range(6):
        pack(k)
        forward(k, 0)
    near_sums()
    weight_tables()
    loads[2].wait()
    t = 0
    for ks in ((0, 1, 2), (3, 4, 5)):
        for step in (1, 3, 2):
            for k in ks:
                forward(k, step)
                if t < 16:
                    local_type(t)
                    t += 1
    loads[3].wait()
    to_slots.wait()
    for k in range(3):
        remote_rows((k,))
    store_rows(0, 48).start()
    far_rows(0, 48)
    remote_rows((3, 4, 5))
    store_rows(48, 16).start()
    far_rows(48, 16)
    store_rows(0, 48).wait()
    store_rows(48, 16).wait()
    for k in range(6):
        drain(finals[k].at[pl.ds(0, 224)], f_send.at[k])
        drain(packed[k].at[pl.ds(0, 3)], s_send.at[k])
        drain(gathered[k].at[pl.ds(0, 96)], g_send.at[k])
    drain(ask_v.at[pl.ds(0, 7)], ask_send.at[0])
    drain(ask_v.at[pl.ds(0, 66)], ask_send.at[1])


def on_device(
    multipoles, translations, local_source, remote_owner, remote_box, charges, positions, leaf_count
):
    any_space = pl.BlockSpec(memory_space=pl.ANY)
    vmem = pl.BlockSpec(memory_space=pltpu.VMEM)
    smem = pl.BlockSpec(memory_space=pltpu.SMEM)
    dma = pltpu.SemaphoreType.DMA
    bf16, f32, i32 = jnp.bfloat16, jnp.float32, jnp.int32
    results = pl.pallas_call(
        whole_kernel,
        out_shape=[
            jax.ShapeDtypeStruct((32, 64, 512), f32),
            jax.ShapeDtypeStruct((64, 2048), f32),
        ]
        + [jax.ShapeDtypeStruct((4, 64, ROWS, part[3]), bf16) for part in PARTS],
        in_specs=[vmem, vmem, smem, smem, any_space, any_space, any_space, any_space],
        out_specs=[any_space, vmem] + [any_space] * 6,
        scratch_shapes=[pltpu.VMEM((128, ROWS, part[3]), bf16) for part in PARTS]
        + [pltpu.VMEM((4, 64, ROWS, part[3]), bf16) for part in PARTS]
        + [pltpu.VMEM((256, ROWS, part[3]), bf16) for part in PARTS]
        + [
            pltpu.VMEM((128, 2, 128), i32),
            pltpu.SMEM((128, 2, 128), i32),
            pltpu.VMEM((8, 256), i32),
            pltpu.SMEM((8, 256), i32),
            pltpu.VMEM((32, 64, 512), bf16),
            pltpu.VMEM((8, 512, 512), bf16),
            pltpu.VMEM((2, 512, 512), bf16),
            pltpu.VMEM((32, 64, 512), f32),
            pltpu.VMEM((512, 512), bf16),
            pltpu.VMEM((64, 2048), bf16),
            pltpu.VMEM((8, 2048), f32),
            pltpu.VMEM((64, 2176), bf16),
            pltpu.VMEM((2176, 8), f32),
            pltpu.VMEM((16, 512, 256), bf16),
            pltpu.VMEM((2, 72, 128), f32),
            pltpu.VMEM((2, 72, 128), f32),
            dma((2,)), dma((2,)), dma((2,)), dma((6,)), dma((6, 3)), dma((6,)), dma((6,)), dma((6, 4)), dma((6,)), dma((6,)), dma((6,)),
            dma((4,)), dma((2,)), dma((2,)), dma((2,)), dma((2,)),
        ],
        compiler_params=pltpu.CompilerParams(collective_id=0, has_side_effects=True, vmem_limit_bytes=62 * 2**20),
    )(remote_owner, remote_box[:, None], local_source, leaf_count, multipoles, translations, charges, positions)
    return results[0], results[1]


def solution(mesh):
    placed = (
        P(("slab", "sub"), None, None),
        P(),
        P(None, ("slab", "sub")),
        P(("slab", "sub"), None),
        P(("slab", "sub")),
        P(None, ("slab", "sub")),
        P(None, ("slab", "sub")),
        P(("slab", "sub")),
    )
    return jax.shard_map(
        on_device,
        mesh=mesh,
        in_specs=placed,
        out_specs=(P(("slab", "sub"), None, None), P(None, ("slab", "sub"))),
        check_vma=False,
    )
```

time: 318 us -> 191 us (0.60)
  matrix products: 55 us -> 0 us
  local copies, waits for them, and re-layouts: 52.1 us -> 8.71 us
  other arithmetic: 27.9 us -> 0 us
  Pallas kernels: 172 us -> 182 us
  starting transfers between devices: 6.52 us -> 0 us
    dot_general x3 -> x0, matrix products: 55 us -> none  [the longest x1 35.8 us: on_device(): jnp.einsum('tbrp,tpq->brq', sources, translations, preferred_element_type...]
    gather x7 -> x0, local copies, waits for them, and re-layouts: 38.4 us -> none  [the longest x6 22.3 us: on_device(): pieces.append(jnp.take(part, slot, axis=0, mode='clip'))]
    concatenate x2 -> x0, other arithmetic: 11.4 us -> none  [the longest x1 11.4 us: on_device(): jnp.concatenate(pieces[:3] + [last], 1)]
    sub x1 -> x0, other arithmetic: 10.3 us -> none  [near_field(): diff = targets[:, :, :, None, None] - source_pos[:, :, None, :, :]]
    pallas_call x1, Pallas kernels: 172 us -> 182 us  [on_device(): pl.pallas_call(whole_kernel, out_shape=[jax.ShapeDtypeStruct((32, 64, 512...]
    mul x2 -> x0, local copies, waits for them, and re-layouts: 8.44 us -> none  [the longest x1 7.83 us: interpolate(): first[:, :, None, None] * second[:, None, :, None] * third[:, None, None, :]]
    ppermute x2 -> x0, starting transfers between devices: 6.52 us -> none  [the longest x1 4.59 us: extended(): lax.ppermute(tail, axis, [(i, (i + 1) % count) for i in range(ends)])]
    unnamed x25 -> x5, local copies, waits for them, and re-layouts: 0.86 us -> 7.24 us
  transfers between devices with their start and end apart: 2 -> 0, of which waited for: 0 -> 0; matrix products, arithmetic and copies ran while one was open for 32% -> 0% of each run, Pallas kernels for 55% -> 0%
where the time goes in v2:
time: 191 us
  Pallas kernels  182 us (95%)
  local copies, waits for them, and re-layouts  8.71 us (5%)
    pallas_call x1, Pallas kernels, on_device(): pl.pallas_call(whole_kernel, out_shape=[jax.ShapeDtypeStruct((32, 64, 512...  182 us
    unnamed x5, local copies, waits for them, and re-layouts  7.24 us

profile of v2, /device:TPU:1, one launch (start us, length us, event | category | flops | bytes accessed | tf_op | source)
XLA Modules:
  0.0 191.0 jit_solution(5944296460323170609)
XLA Ops:
  0.6 1.5 copy.11.owner_ref
  2.1 1.5 copy.12.box_ref
  3.6 181.6 %shard_map.95 = (f32[32,64,512]{2,1,0:T(8,128)}, f32[64,2048]{1,0:T(8,128)}, bf16[4,64,16,512]{3,2,1,0:T(8,128)(2,1)}, bf16[4,64,16,512]{3,2,1,0:T(8,128)(2,1)},...) custom-call(s32[256,1]{1,0:T(8,128)} %copy.11.owner_ref, ...), custom_call_target="tpu_custom_call" | custom-call | tf_op jit(solution)/shard_map/pallas_call | solution.py:388
  185.2 0.0 copy-start
  185.2 5.0 %copy.15 = f32[32,64,512]{2,1,0:T(8,128)} copy(f32[32,64,512]{2,1,0:T(8,128)} %get-tuple-element.8) | data formatting | bytes 8388608
  190.2 0.0 copy-done
  190.2 0.8 copy.16
Async XLA Ops:
  185.2 5.0 %copy-start = (f32[64,2048]{1,0:T(8,128)S(1)}, f32[64,2048]{1,0:T(8,128)}, u32[]{:S(2)}) copy-start(f32[64,2048]{1,0:T(8,128)} %get-tuple-element.9) | copy-start | bytes 1572868

commit v3 on v2

--- a/solution.py
+++ b/solution.py
@@ -41,19 +41,25 @@
 
 
 def whole_kernel(
-    owner_ref, box_ref, local_ref, count_ref, mult_ref, ops_ref, charge_ref, pos_ref, expansion_ref, potential_ref, *scratch
+    owner_ref, box_ref, local_hbm, count_hbm, mult_ref, ops_ref, charge_ref, pos_ref, expansion_ref, potential_ref, *scratch
 ):
     relay, scratch = scratch[0:6], scratch[6:]
     gathered, packed, finals = scratch[0:6], scratch[6:12], scratch[12:18]
     ask_v, ask_s, slot_v, slot_s = scratch[18:22]
     mult, ops, stream, total, lhs, charges, places, shifted, columns, tables, edge_out, edge_in = scratch[22:34]
+    asked, local_ref, count_ref = scratch[34:37]
+    scratch = scratch[0:34] + scratch[37:]
     (ask_send, ask_recv, copy_sem, g_send, g_recv, g_own, s_send, s_recv, f_send, f_recv, f_own) = scratch[34:45]
     load_sem, stream_sem, edge_send, edge_recv, out_sem = scratch[45:]
     loads = [
+        pltpu.make_async_copy(local_hbm, local_ref, load_sem.at[4]),
+        pltpu.make_async_copy(count_hbm, count_ref, load_sem.at[5]),
+        pltpu.make_async_copy(owner_ref, asked.at[0], load_sem.at[6]),
+        pltpu.make_async_copy(box_ref, asked.at[1], load_sem.at[7]),
         pltpu.make_async_copy(charge_ref, charges, load_sem.at[0]),
         pltpu.make_async_copy(pos_ref, places.at[pl.ds(0, 3)], load_sem.at[1]),
         pltpu.make_async_copy(mult_ref, mult, load_sem.at[2]),
-        pltpu.make_async_copy(ops_ref.at[pl.ds(16, 8)], ops, load_sem.at[3]),
+        pltpu.make_async_copy(ops_ref.at[pl.ds(4, 2)], ops, load_sem.at[3]),
     ]
     places[...] = jnp.zeros_like(places)
     for load in loads:
@@ -78,11 +84,15 @@
     for number in (after, prior):
         pl.semaphore_signal(barrier, 1, device_id=(number // 8, number % 8), device_id_type=MESH)
 
-    owner, box = owner_ref[...], box_ref[...]
-    rows = owner.shape[0]
+    loads[2].wait()
+    loads[3].wait()
+    rows = 256
     down = lax.broadcasted_iota(jnp.int32, (rows, rows), 0)
     along = lax.broadcasted_iota(jnp.int32, (rows, rows), 1)
-    across = jnp.sum(jnp.where(down == along, owner, 0), axis=0, keepdims=True)
+    across = jnp.concatenate([asked[0, 0:1, :], asked[0, 1:2, :]], 1)
+    boxes_across = jnp.concatenate([asked[1, 0:1, :], asked[1, 1:2, :]], 1)
+    owner = jnp.sum(jnp.where(down == along, across, 0), axis=1, keepdims=True)
+    box = jnp.sum(jnp.where(down == along, boxes_across, 0), axis=1, keepdims=True)
     before = jnp.where((owner == across) & (along < down), 1, 0)
     rank = jnp.sum(before, axis=1, keepdims=True)
     row_rank = jnp.sum(jnp.where((owner == across) & (down < along), 1, 0), axis=0, keepdims=True)
@@ -121,8 +131,9 @@
         return jnp.where(present(i), charges[:, tile(i)].astype(jnp.float32), 0.0)
 
     def send_edges():
-        loads[0].wait()
         loads[1].wait()
+        loads[4].wait()
+        loads[5].wait()
         for way, (i, number) in enumerate(((15, after), (0, prior))):
             edge_out[way, 0:64, :] = masked(i)
             edge_out[way, 64:72, :] = places[:, tile(i)]
@@ -142,8 +153,28 @@
             row = ask_v.at[pl.ds(mine, 1)]
             send(row, row, ask_send.at[0], ask_recv.at[0], moved(me, "y", step), c)
 
+    def boxes_of(k, at, first, count):
+        return gathered[k].at[pl.ds(at[ORDERS[PARTS[k][0]][0]] * 32 + first, count)]
+
+    def spread(k, first, count, step, sem):
+        order, r0, c0, cols = PARTS[k]
+        src = mult_ref.at[pl.ds(first, count), pl.ds(r0, ROWS), pl.ds(c0, cols)]
+        dst = boxes_of(k, me, first, count)
+        send(src, dst, g_send.at[k], g_recv.at[k, sem], moved(me, ORDERS[order][0], step), core)
+
+    def pass_on(k):
+        axis = ORDERS[PARTS[k][0]][0]
+        for way, step in ((0, 3), (1, 1)):
+            came = moved(me, axis, step)
+            half = boxes_of(k, came, 16 * way, 16)
+            drain(half, g_recv.at[k, way])
+            send(half, half, g_send.at[k], g_recv.at[k, 2], moved(me, axis, 4 - step), core)
+
+    for k in range(3):
+        spread(k, 0, 16, 1, 0)
+        spread(k, 16, 16, 3, 1)
+    send_edges()
     drain(ask_v.at[pl.ds(0, 7)], ask_recv.at[0])
-    send_edges()
     for step in (1, 3, 2):
         part = ask_v.at[pl.ds(slab * 8, 8)]
         send(part, part, ask_send.at[1], ask_recv.at[1], moved(me, "z", step), core)
@@ -152,35 +183,28 @@
         for x in (1, 3, 2):
             part = ask_v.at[pl.ds(slab * 8 + me["y"] * 2, 2)]
             send(part, part, ask_send.at[1], ask_recv.at[1], moved(moved(me, "z", z), "x", x), core)
-
-    def boxes_of(k, at, first, count):
-        return gathered[k].at[pl.ds(at[ORDERS[PARTS[k][0]][0]] * 32 + first, count)]
-
+    for k in range(3):
+        spread(k, 16, 16, 1, 2)
+        spread(k, 0, 16, 3, 2)
     for k, (order, r0, c0, cols) in enumerate(PARTS):
-        axis = ORDERS[order][0]
-        src = mult_ref.at[:, pl.ds(r0, ROWS), pl.ds(c0, cols)]
-        dst = boxes_of(k, me, 0, 32)
-        send(src, dst, g_send.at[k], g_recv.at[k, 0], moved(me, axis, 1), core)
-        send(src, dst, g_send.at[k], g_recv.at[k, 1], moved(me, axis, 3), core)
-        pltpu.make_async_copy(src, dst, g_own.at[k]).start()
+        own_boxes = mult_ref.at[:, pl.ds(r0, ROWS), pl.ds(c0, cols)]
+        pltpu.make_async_copy(own_boxes, boxes_of(k, me, 0, 32), g_own.at[k]).start()
+    for k in range(3):
+        pass_on(k)
+    for k in range(3, 6):
+        spread(k, 0, 16, 1, 0)
+        spread(k, 16, 16, 3, 1)
+        spread(k, 16, 16, 1, 2)
+        spread(k, 0, 16, 3, 2)
     drain(ask_v.at[pl.ds(0, 66)], ask_recv.at[1])
     to_scalars = pltpu.make_async_copy(ask_v, ask_s, copy_sem.at[0])
     to_scalars.start()
-    for k in range(6):
-        axis = ORDERS[PARTS[k][0]][0]
-        for way, step in ((0, 3), (1, 1)):
-            came = moved(me, axis, step)
-            drain(boxes_of(k, came, 0, 32), g_recv.at[k, way])
-            half = boxes_of(k, came, 16 * way, 16)
-            send(half, half, g_send.at[k], g_recv.at[k, 2], moved(me, axis, 4 - step), core)
     to_scalars.wait()
 
-    def pack(k):
+    def pack(k, steps):
         order, r0, c0, cols = PARTS[k]
         g, p, q = ORDERS[order]
-        drain(gathered[k].at[pl.ds(0, 32)], g_recv.at[k, 2])
-        drain(gathered[k].at[pl.ds(0, 32)], g_own.at[k])
-        for step in (1, 3, 2, 0):
+        for step in steps:
             target = moved(me, p, step)
 
             def one(j, _):
@@ -198,6 +222,10 @@
             lax.fori_loop(0, 32, one, 0, unroll=4)
             if step:
                 send(packed[k].at[target[p]], relay[k].at[me[p]], s_send.at[k], s_recv.at[k, me[p]], target, core)
+
+    def boxes_are_here(k):
+        drain(gathered[k].at[pl.ds(0, 64)], g_recv.at[k, 2])
+        drain(gathered[k].at[pl.ds(0, 32)], g_own.at[k])
 
     def forward(k, step):
         order = PARTS[k][0]
@@ -289,7 +317,9 @@
         lax.fori_loop(0, 16, pair, 0)
 
     def load_op(t):
-        return pltpu.make_async_copy(ops_ref.at[t], stream.at[t % 2], stream_sem.at[t % 2])
+        return pltpu.make_async_copy(
+            ops_ref.at[t // 4, pl.ds(t % 4 * 512, 512)], stream.at[t % 2], stream_sem.at[t % 2]
+        )
 
     def local_type(t):
         load_op(t).wait()
@@ -298,8 +328,8 @@
 
         def group(i, _):
             for b in range(8):
-                lhs[b * 64 : b * 64 + 64, :] = mult[local_ref[t, i * 8 + b]]
-            value = dot(lhs[...], stream[t % 2]).reshape(8, 64, 512)
+                lhs[b * 64 : b * 64 + 64, 0:512] = mult[local_ref[t, i * 8 + b]]
+            value = dot(lhs[:, 0:512], stream[t % 2]).reshape(8, 64, 512)
             if t == 0:
                 total[pl.ds(i * 8, 8)] = value
             else:
@@ -315,15 +345,16 @@
             drain(finals[k].at[pl.ds(0, 32)], f_own.at[k])
 
         def one(t, _):
-            at = 0
             for k in parts:
                 order, _, c0, cols = PARTS[k]
-                for b in range(32):
-                    lhs[b * 16 : b * 16 + 16, c0 : c0 + cols] = finals[k][slot_s[order, t * 32 + b]]
+                for half in range(4):
+                    for b in range(32):
+                        at = pl.ds(half * 512 + c0, cols)
+                        lhs[b * 16 : b * 16 + 16, at] = finals[k][slot_s[order, (4 * t + half) * 32 + b]]
             total[:, r0 : r0 + ROWS, :] += dot(lhs[...], ops[t]).reshape(32, ROWS, 512)
             return 0
 
-        lax.fori_loop(0, 8, one, 0)
+        lax.fori_loop(0, 2, one, 0)
 
     def store_rows(r0, count):
         return pltpu.make_async_copy(
@@ -335,7 +366,7 @@
             value = total[pl.ds(2 * i, 2), r0 : r0 + count, :].reshape(2 * count, 512)
             high, low = split(value)
             both = dot(jnp.concatenate([high, low], 0), tables[i])
-            summed = both[: 2 * count, 0:128] + both[: 2 * count, 128:256] + both[2 * count :, 0:128]
+            summed = (both[: 2 * count, 0:128] + both[: 2 * count, 128:256]) + (both[2 * count :, 0:128] + both[2 * count :, 128:256])
             far = jnp.where(second, summed[count:], summed[:count])
             near = potential_ref[r0 : r0 + count, tile(i)]
             potential_ref[r0 : r0 + count, tile(i)] = jnp.where(present(i), near + far, 0.0)
@@ -344,21 +375,32 @@
         lax.fori_loop(0, 16, pair, 0)
 
     load_op(0).start()
-    for k in range(6):
-        pack(k)
-        forward(k, 0)
+    for k in range(3):
+        boxes_are_here(k)
+        pack(k, (1, 3))
+    for k in range(3, 6):
+        pass_on(k)
+    for k in range(3):
+        pack(k, (2, 0))
     near_sums()
     weight_tables()
-    loads[2].wait()
-    t = 0
+    loads[0].wait()
+    loads[6].wait()
+    for t in range(4):
+        local_type(t)
+    for k in range(3, 6):
+        boxes_are_here(k)
+        pack(k, (1, 3, 2, 0))
+    t = 4
     for ks in ((0, 1, 2), (3, 4, 5)):
-        for step in (1, 3, 2):
+        for step in (0, 1, 3, 2):
             for k in ks:
                 forward(k, step)
-                if t < 16:
-                    local_type(t)
-                    t += 1
-    loads[3].wait()
+            if t < 16:
+                local_type(t)
+                local_type(t + 1)
+                t += 2
+    loads[7].wait()
     to_slots.wait()
     for k in range(3):
         remote_rows((k,))
@@ -382,7 +424,6 @@
 ):
     any_space = pl.BlockSpec(memory_space=pl.ANY)
     vmem = pl.BlockSpec(memory_space=pltpu.VMEM)
-    smem = pl.BlockSpec(memory_space=pltpu.SMEM)
     dma = pltpu.SemaphoreType.DMA
     bf16, f32, i32 = jnp.bfloat16, jnp.float32, jnp.int32
     results = pl.pallas_call(
@@ -392,7 +433,7 @@
             jax.ShapeDtypeStruct((64, 2048), f32),
         ]
         + [jax.ShapeDtypeStruct((4, 64, ROWS, part[3]), bf16) for part in PARTS],
-        in_specs=[vmem, vmem, smem, smem, any_space, any_space, any_space, any_space],
+        in_specs=[any_space] * 8,
         out_specs=[any_space, vmem] + [any_space] * 6,
         scratch_shapes=[pltpu.VMEM((128, ROWS, part[3]), bf16) for part in PARTS]
         + [pltpu.VMEM((4, 64, ROWS, part[3]), bf16) for part in PARTS]
@@ -403,10 +444,10 @@
             pltpu.VMEM((8, 256), i32),
             pltpu.SMEM((8, 256), i32),
             pltpu.VMEM((32, 64, 512), bf16),
-            pltpu.VMEM((8, 512, 512), bf16),
+            pltpu.VMEM((2, 2048, 512), bf16),
             pltpu.VMEM((2, 512, 512), bf16),
             pltpu.VMEM((32, 64, 512), f32),
-            pltpu.VMEM((512, 512), bf16),
+            pltpu.VMEM((512, 2048), bf16),
             pltpu.VMEM((64, 2048), bf16),
             pltpu.VMEM((8, 2048), f32),
             pltpu.VMEM((64, 2176), bf16),
@@ -414,11 +455,14 @@
             pltpu.VMEM((16, 512, 256), bf16),
             pltpu.VMEM((2, 72, 128), f32),
             pltpu.VMEM((2, 72, 128), f32),
+            pltpu.VMEM((2, 2, 128), i32),
+            pltpu.SMEM((16, 32), i32),
+            pltpu.SMEM((32,), i32),
             dma((2,)), dma((2,)), dma((2,)), dma((6,)), dma((6, 3)), dma((6,)), dma((6,)), dma((6, 4)), dma((6,)), dma((6,)), dma((6,)),
-            dma((4,)), dma((2,)), dma((2,)), dma((2,)), dma((2,)),
+            dma((8,)), dma((2,)), dma((2,)), dma((2,)), dma((2,)),
         ],
         compiler_params=pltpu.CompilerParams(collective_id=0, has_side_effects=True, vmem_limit_bytes=62 * 2**20),
-    )(remote_owner, remote_box[:, None], local_source, leaf_count, multipoles, translations, charges, positions)
+    )(remote_owner.reshape(2, 128), remote_box.reshape(2, 128), local_source, leaf_count, multipoles, translations.reshape(6, 2048, 512), charges, positions)
     return results[0], results[1]
 
 

time: 191 us -> 174 us (0.911)
  Pallas kernels: 182 us -> 168 us
  local copies, waits for them, and re-layouts: 8.71 us -> 5.77 us
    pallas_call x1, Pallas kernels: 182 us -> 168 us  [on_device(): pl.pallas_call(whole_kernel, out_shape=[jax.ShapeDtypeStruct((32, 64, 512...]
    unnamed x5 -> x4, local copies, waits for them, and re-layouts: 7.24 us -> 5.77 us
where the time goes in v3:
time: 174 us
  Pallas kernels  168 us (97%)
  local copies, waits for them, and re-layouts  5.77 us (3%)
    pallas_call x1, Pallas kernels, on_device(): pl.pallas_call(whole_kernel, out_shape=[jax.ShapeDtypeStruct((32, 64, 512...  168 us
    unnamed x4, local copies, waits for them, and re-layouts  5.77 us

profile of v3, /device:TPU:1, one launch (start us, length us, event | category | flops | bytes accessed | tf_op | source)
XLA Modules:
  0.0 174.2 jit_solution(9238622481301581711)
XLA Ops:
  0.6 167.8 %shard_map.95 = (f32[32,64,512]{2,1,0:T(8,128)}, f32[64,2048]{1,0:T(8,128)}, bf16[4,64,16,512]{3,2,1,0:T(8,128)(2,1)}, bf16[4,64,16,512]{3,2,1,0:T(8,128)(2,1)},...) custom-call(s32[2,128]{1,0:T(2,128)} %bitcast.4, ...), custom_call_target="tpu_custom_call" | custom-call | tf_op jit(solution)/shard_map/pallas_call | solution.py:429
  168.5 0.0 copy-start
  168.5 5.0 %copy.12 = f32[32,64,512]{2,1,0:T(8,128)} copy(f32[32,64,512]{2,1,0:T(8,128)} %get-tuple-element.8) | data formatting | bytes 8388608
  173.4 0.0 copy-done
  173.4 0.8 copy.13
Async XLA Ops:
  168.5 5.0 %copy-start = (f32[64,2048]{1,0:T(8,128)S(1)}, f32[64,2048]{1,0:T(8,128)}, u32[]{:S(2)}) copy-start(f32[64,2048]{1,0:T(8,128)} %get-tuple-element.9) | copy-start | bytes 1572868

commit v4 on v3

--- a/solution.py
+++ b/solution.py
@@ -46,24 +46,12 @@
     relay, scratch = scratch[0:6], scratch[6:]
     gathered, packed, finals = scratch[0:6], scratch[6:12], scratch[12:18]
     ask_v, ask_s, slot_v, slot_s = scratch[18:22]
-    mult, ops, stream, total, lhs, charges, places, shifted, columns, tables, edge_out, edge_in = scratch[22:34]
-    asked, local_ref, count_ref = scratch[34:37]
-    scratch = scratch[0:34] + scratch[37:]
-    (ask_send, ask_recv, copy_sem, g_send, g_recv, g_own, s_send, s_recv, f_send, f_recv, f_own) = scratch[34:45]
-    load_sem, stream_sem, edge_send, edge_recv, out_sem = scratch[45:]
-    loads = [
-        pltpu.make_async_copy(local_hbm, local_ref, load_sem.at[4]),
-        pltpu.make_async_copy(count_hbm, count_ref, load_sem.at[5]),
-        pltpu.make_async_copy(owner_ref, asked.at[0], load_sem.at[6]),
-        pltpu.make_async_copy(box_ref, asked.at[1], load_sem.at[7]),
-        pltpu.make_async_copy(charge_ref, charges, load_sem.at[0]),
-        pltpu.make_async_copy(pos_ref, places.at[pl.ds(0, 3)], load_sem.at[1]),
-        pltpu.make_async_copy(mult_ref, mult, load_sem.at[2]),
-        pltpu.make_async_copy(ops_ref.at[pl.ds(4, 2)], ops, load_sem.at[3]),
-    ]
-    places[...] = jnp.zeros_like(places)
-    for load in loads:
-        load.start()
+    mult, ops, stream, lhs, charges, places, shifted, columns, tables, edge_out, edge_in = scratch[22:33]
+    asked, local_ref, count_ref = scratch[33:36]
+    total = expansion_ref
+    scratch = scratch[0:33] + scratch[36:]
+    (ask_send, ask_recv, copy_sem, g_send, g_recv, g_own, s_send, s_recv, f_send, f_recv, f_own) = scratch[33:44]
+    load_sem, stream_sem, edge_send, edge_recv = scratch[44:]
     slab, sub = lax.axis_index("slab"), lax.axis_index("sub")
     me = {"x": slab // 4, "y": sub // 2, "z": slab % 4}
     core = sub % 2
@@ -84,6 +72,77 @@
     for number in (after, prior):
         pl.semaphore_signal(barrier, 1, device_id=(number // 8, number % 8), device_id_type=MESH)
 
+    loads = [
+        pltpu.make_async_copy(local_hbm, local_ref, load_sem.at[4]),
+        pltpu.make_async_copy(count_hbm, count_ref, load_sem.at[5]),
+        pltpu.make_async_copy(owner_ref, asked.at[0], load_sem.at[6]),
+        pltpu.make_async_copy(box_ref, asked.at[1], load_sem.at[7]),
+        pltpu.make_async_copy(charge_ref, charges, load_sem.at[0]),
+        pltpu.make_async_copy(pos_ref, places.at[pl.ds(0, 3)], load_sem.at[1]),
+        pltpu.make_async_copy(mult_ref, mult, load_sem.at[2]),
+        pltpu.make_async_copy(ops_ref.at[pl.ds(4, 2)], ops, load_sem.at[3]),
+    ]
+    places[...] = jnp.zeros_like(places)
+    for load in loads:
+        load.start()
+    pl.semaphore_wait(barrier, len(partners) + 2)
+
+    def send(src, dst, ssem, rsem, at, c):
+        pltpu.make_async_remote_copy(
+            src_ref=src, dst_ref=dst, send_sem=ssem, recv_sem=rsem, device_id=place(at, c), device_id_type=MESH
+        ).start()
+
+    def drain(ref, sem):
+        pltpu.make_async_copy(ref, ref, sem).wait()
+
+    lane = lax.broadcasted_iota(jnp.int32, (1, 128), 1)
+    second = lane >= 64
+
+    def tile(i):
+        return pl.ds(pl.multiple_of(i * 128, 128), 128)
+
+    def present(i):
+        return (lane % 64) < jnp.where(second, count_ref[2 * i + 1], count_ref[2 * i])
+
+    def masked(i):
+        return jnp.where(present(i), charges[:, tile(i)].astype(jnp.float32), 0.0)
+
+    def send_edges():
+        loads[1].wait()
+        loads[4].wait()
+        loads[5].wait()
+        for way, (i, number) in enumerate(((15, after), (0, prior))):
+            edge_out[way, 0:64, :] = masked(i)
+            edge_out[way, 64:72, :] = places[:, tile(i)]
+            pltpu.make_async_remote_copy(
+                src_ref=edge_out.at[way],
+                dst_ref=edge_in.at[way],
+                send_sem=edge_send.at[way],
+                recv_sem=edge_recv.at[way],
+                device_id=(number // 8, number % 8),
+                device_id_type=MESH,
+            ).start()
+
+    def boxes_of(k, at, first, count):
+        return gathered[k].at[pl.ds(at[ORDERS[PARTS[k][0]][0]] * 32 + first, count)]
+
+    def spread(k, first, count, step, sem):
+        order, r0, c0, cols = PARTS[k]
+        src = mult_ref.at[pl.ds(first, count), pl.ds(r0, ROWS), pl.ds(c0, cols)]
+        dst = boxes_of(k, me, first, count)
+        send(src, dst, g_send.at[k], g_recv.at[k, sem], moved(me, ORDERS[order][0], step), core)
+
+    def pass_on(k):
+        axis = ORDERS[PARTS[k][0]][0]
+        for way, step in ((0, 3), (1, 1)):
+            came = moved(me, axis, step)
+            half = boxes_of(k, came, 16 * way, 16)
+            drain(half, g_recv.at[k, way])
+            send(half, half, g_send.at[k], g_recv.at[k, 2], moved(me, axis, 4 - step), core)
+
+    for k in range(3):
+        spread(k, 0, 16, 1, 0)
+        spread(k, 16, 16, 3, 1)
     loads[2].wait()
     loads[3].wait()
     rows = 256
@@ -108,44 +167,6 @@
         wanted = jnp.sum(jnp.where(named & (rank == r), box, 0), axis=0, keepdims=True)
         ask_v[mine, r : r + 1, :] = wanted
 
-    pl.semaphore_wait(barrier, len(partners) + 2)
-
-    def send(src, dst, ssem, rsem, at, c):
-        pltpu.make_async_remote_copy(
-            src_ref=src, dst_ref=dst, send_sem=ssem, recv_sem=rsem, device_id=place(at, c), device_id_type=MESH
-        ).start()
-
-    def drain(ref, sem):
-        pltpu.make_async_copy(ref, ref, sem).wait()
-
-    lane = lax.broadcasted_iota(jnp.int32, (1, 128), 1)
-    second = lane >= 64
-
-    def tile(i):
-        return pl.ds(pl.multiple_of(i * 128, 128), 128)
-
-    def present(i):
-        return (lane % 64) < jnp.where(second, count_ref[2 * i + 1], count_ref[2 * i])
-
-    def masked(i):
-        return jnp.where(present(i), charges[:, tile(i)].astype(jnp.float32), 0.0)
-
-    def send_edges():
-        loads[1].wait()
-        loads[4].wait()
-        loads[5].wait()
-        for way, (i, number) in enumerate(((15, after), (0, prior))):
-            edge_out[way, 0:64, :] = masked(i)
-            edge_out[way, 64:72, :] = places[:, tile(i)]
-            pltpu.make_async_remote_copy(
-                src_ref=edge_out.at[way],
-                dst_ref=edge_in.at[way],
-                send_sem=edge_send.at[way],
-                recv_sem=edge_recv.at[way],
-                device_id=(number // 8, number % 8),
-                device_id_type=MESH,
-            ).start()
-
     for step in (0, 1, 3, 2):
         for c in (core, 1 - core):
             if step == 0 and c is core:
@@ -153,26 +174,9 @@
             row = ask_v.at[pl.ds(mine, 1)]
             send(row, row, ask_send.at[0], ask_recv.at[0], moved(me, "y", step), c)
 
-    def boxes_of(k, at, first, count):
-        return gathered[k].at[pl.ds(at[ORDERS[PARTS[k][0]][0]] * 32 + first, count)]
-
-    def spread(k, first, count, step, sem):
-        order, r0, c0, cols = PARTS[k]
-        src = mult_ref.at[pl.ds(first, count), pl.ds(r0, ROWS), pl.ds(c0, cols)]
-        dst = boxes_of(k, me, first, count)
-        send(src, dst, g_send.at[k], g_recv.at[k, sem], moved(me, ORDERS[order][0], step), core)
-
-    def pass_on(k):
-        axis = ORDERS[PARTS[k][0]][0]
-        for way, step in ((0, 3), (1, 1)):
-            came = moved(me, axis, step)
-            half = boxes_of(k, came, 16 * way, 16)
-            drain(half, g_recv.at[k, way])
-            send(half, half, g_send.at[k], g_recv.at[k, 2], moved(me, axis, 4 - step), core)
-
-    for k in range(3):
-        spread(k, 0, 16, 1, 0)
-        spread(k, 16, 16, 3, 1)
+    for k in range(3):
+        spread(k, 16, 16, 1, 2)
+        spread(k, 0, 16, 3, 2)
     send_edges()
     drain(ask_v.at[pl.ds(0, 7)], ask_recv.at[0])
     for step in (1, 3, 2):
@@ -183,9 +187,6 @@
         for x in (1, 3, 2):
             part = ask_v.at[pl.ds(slab * 8 + me["y"] * 2, 2)]
             send(part, part, ask_send.at[1], ask_recv.at[1], moved(moved(me, "z", z), "x", x), core)
-    for k in range(3):
-        spread(k, 16, 16, 1, 2)
-        spread(k, 0, 16, 3, 2)
     for k, (order, r0, c0, cols) in enumerate(PARTS):
         own_boxes = mult_ref.at[:, pl.ds(r0, ROWS), pl.ds(c0, cols)]
         pltpu.make_async_copy(own_boxes, boxes_of(k, me, 0, 32), g_own.at[k]).start()
@@ -356,11 +357,6 @@
 
         lax.fori_loop(0, 2, one, 0)
 
-    def store_rows(r0, count):
-        return pltpu.make_async_copy(
-            total.at[:, pl.ds(r0, count)], expansion_ref.at[:, pl.ds(r0, count)], out_sem.at[r0 // 48]
-        )
-
     def far_rows(r0, count):
         def pair(i, _):
             value = total[pl.ds(2 * i, 2), r0 : r0 + count, :].reshape(2 * count, 512)
@@ -372,16 +368,16 @@
             potential_ref[r0 : r0 + count, tile(i)] = jnp.where(present(i), near + far, 0.0)
             return 0
 
-        lax.fori_loop(0, 16, pair, 0)
+        lax.fori_loop(0, 16, pair, 0, unroll=8)
 
     load_op(0).start()
     for k in range(3):
         boxes_are_here(k)
-        pack(k, (1, 3))
+        pack(k, (2,))
     for k in range(3, 6):
         pass_on(k)
     for k in range(3):
-        pack(k, (2, 0))
+        pack(k, (1, 3, 0))
     near_sums()
     weight_tables()
     loads[0].wait()
@@ -404,13 +400,9 @@
     to_slots.wait()
     for k in range(3):
         remote_rows((k,))
-    store_rows(0, 48).start()
     far_rows(0, 48)
     remote_rows((3, 4, 5))
-    store_rows(48, 16).start()
     far_rows(48, 16)
-    store_rows(0, 48).wait()
-    store_rows(48, 16).wait()
     for k in range(6):
         drain(finals[k].at[pl.ds(0, 224)], f_send.at[k])
         drain(packed[k].at[pl.ds(0, 3)], s_send.at[k])
@@ -429,12 +421,12 @@
     results = pl.pallas_call(
         whole_kernel,
         out_shape=[
-            jax.ShapeDtypeStruct((32, 64, 512), f32),
-            jax.ShapeDtypeStruct((64, 2048), f32),
+            pltpu.VMEM((32, 64, 512), f32),
+            pltpu.VMEM((64, 2048), f32),
         ]
         + [jax.ShapeDtypeStruct((4, 64, ROWS, part[3]), bf16) for part in PARTS],
         in_specs=[any_space] * 8,
-        out_specs=[any_space, vmem] + [any_space] * 6,
+        out_specs=[vmem, vmem] + [any_space] * 6,
         scratch_shapes=[pltpu.VMEM((128, ROWS, part[3]), bf16) for part in PARTS]
         + [pltpu.VMEM((4, 64, ROWS, part[3]), bf16) for part in PARTS]
         + [pltpu.VMEM((256, ROWS, part[3]), bf16) for part in PARTS]
@@ -446,7 +438,6 @@
             pltpu.VMEM((32, 64, 512), bf16),
             pltpu.VMEM((2, 2048, 512), bf16),
             pltpu.VMEM((2, 512, 512), bf16),
-            pltpu.VMEM((32, 64, 512), f32),
             pltpu.VMEM((512, 2048), bf16),
             pltpu.VMEM((64, 2048), bf16),
             pltpu.VMEM((8, 2048), f32),
@@ -459,9 +450,9 @@
             pltpu.SMEM((16, 32), i32),
             pltpu.SMEM((32,), i32),
             dma((2,)), dma((2,)), dma((2,)), dma((6,)), dma((6, 3)), dma((6,)), dma((6,)), dma((6, 4)), dma((6,)), dma((6,)), dma((6,)),
-            dma((8,)), dma((2,)), dma((2,)), dma((2,)), dma((2,)),
+            dma((8,)), dma((2,)), dma((2,)), dma((2,)),
         ],
-        compiler_params=pltpu.CompilerParams(collective_id=0, has_side_effects=True, vmem_limit_bytes=62 * 2**20),
+        compiler_params=pltpu.CompilerParams(collective_id=0, has_side_effects=True, vmem_limit_bytes=57 * 2**20),
     )(remote_owner.reshape(2, 128), remote_box.reshape(2, 128), local_source, leaf_count, multipoles, translations.reshape(6, 2048, 512), charges, positions)
     return results[0], results[1]
 

time: 174 us -> 165 us (0.948)
  Pallas kernels: 168 us -> 161 us
  local copies, waits for them, and re-layouts: 5.77 us -> 2.81 us
    pallas_call x1, Pallas kernels: 168 us -> 161 us  [on_device(): pl.pallas_call(whole_kernel, out_shape=[pltpu.VMEM((32, 64, 512), f32), p...]
    unnamed x4 -> x2, local copies, waits for them, and re-layouts: 5.77 us -> 2.81 us
where the time goes in v4:
time: 165 us
  Pallas kernels  161 us (98%)
  local copies, waits for them, and re-layouts  2.81 us (2%)
    pallas_call x1, Pallas kernels, on_device(): pl.pallas_call(whole_kernel, out_shape=[pltpu.VMEM((32, 64, 512), f32), p...  161 us

profile of v4, /device:TPU:1, one launch (start us, length us, event | category | flops | bytes accessed | tf_op | source)
XLA Modules:
  0.0 164.8 jit_solution(824110980797900388)
XLA Ops:
  0.6 161.3 %shard_map.95 = (f32[32,64,512]{2,1,0:T(8,128)S(1)}, f32[64,2048]{1,0:T(8,128)S(1)}, bf16[4,64,16,512]{3,2,1,0:T(8,128)(2,1)}, bf16[4,64,16,512]{3,2,1,0:T(8,128...) custom-call(s32[2,128]{1,0:T(2,128)} %bitcast.4, ...), custom_call_target="tpu_custom_call" | custom-call | tf_op jit(solution)/shard_map/pallas_call | solution.py:421
  162.0 2.0 %copy.12 = f32[32,64,512]{2,1,0:T(8,128)} copy(f32[32,64,512]{2,1,0:T(8,128)S(1)} %get-tuple-element.6) | data formatting | bytes 8388608
  164.0 0.8 copy.13

commit v5 on v4

--- a/solution.py
+++ b/solution.py
@@ -13,6 +13,7 @@
 MESH = pl.DeviceIdType.MESH
 
 PARTS = ((0, 0, 0, 512), (1, 16, 0, 512), (2, 32, 0, 512), (0, 48, 0, 128), (1, 48, 128, 128), (2, 48, 256, 256))
+STARTS = (0, 512, 1024)
 ORDERS = ("xyz", "yzx", "zxy")
 ROWS = 16
 
@@ -40,18 +41,34 @@
     return high, (value - high.astype(jnp.float32)).astype(jnp.bfloat16)
 
 
+def add_far(values, r0, count, tables, potentials):
+    def pair(i, _):
+        value = values[pl.ds(2 * i, 2), r0 : r0 + count, :].reshape(2 * count, 512)
+        high, low = split(value)
+        both = dot(jnp.concatenate([high, low], 0), tables[i])
+        summed = (both[: 2 * count, 0:128] + both[: 2 * count, 128:256]) + (
+            both[2 * count :, 0:128] + both[2 * count :, 128:256]
+        )
+        second = lax.broadcasted_iota(jnp.int32, (1, 128), 1) >= 64
+        at = pl.ds(pl.multiple_of(i * 128, 128), 128)
+        potentials[0:count, at] += jnp.where(second, summed[count:], summed[:count])
+        return 0
+
+    lax.fori_loop(0, 16, pair, 0, unroll=8)
+
+
 def whole_kernel(
     owner_ref, box_ref, local_hbm, count_hbm, mult_ref, ops_ref, charge_ref, pos_ref, expansion_ref, potential_ref, *scratch
 ):
-    relay, scratch = scratch[0:6], scratch[6:]
+    tables, ops, last = scratch[0:3]
+    relay, scratch = scratch[3:9], scratch[9:]
     gathered, packed, finals = scratch[0:6], scratch[6:12], scratch[12:18]
     ask_v, ask_s, slot_v, slot_s = scratch[18:22]
-    mult, ops, stream, lhs, charges, places, shifted, columns, tables, edge_out, edge_in = scratch[22:33]
-    asked, local_ref, count_ref = scratch[33:36]
+    mult, stream, lhs, charges, places, shifted, columns, edge_out, edge_in = scratch[22:31]
+    asked, local_ref, count_ref = scratch[31:34]
     total = expansion_ref
-    scratch = scratch[0:33] + scratch[36:]
-    (ask_send, ask_recv, copy_sem, g_send, g_recv, g_own, s_send, s_recv, f_send, f_recv, f_own) = scratch[33:44]
-    load_sem, stream_sem, edge_send, edge_recv = scratch[44:]
+    (ask_send, ask_recv, copy_sem, g_send, g_recv, g_own, s_send, s_recv, f_send, f_recv, f_own) = scratch[34:45]
+    load_sem, stream_sem, edge_send, edge_recv = scratch[45:]
     slab, sub = lax.axis_index("slab"), lax.axis_index("sub")
     me = {"x": slab // 4, "y": sub // 2, "z": slab % 4}
     core = sub % 2
@@ -72,19 +89,6 @@
     for number in (after, prior):
         pl.semaphore_signal(barrier, 1, device_id=(number // 8, number % 8), device_id_type=MESH)
 
-    loads = [
-        pltpu.make_async_copy(local_hbm, local_ref, load_sem.at[4]),
-        pltpu.make_async_copy(count_hbm, count_ref, load_sem.at[5]),
-        pltpu.make_async_copy(owner_ref, asked.at[0], load_sem.at[6]),
-        pltpu.make_async_copy(box_ref, asked.at[1], load_sem.at[7]),
-        pltpu.make_async_copy(charge_ref, charges, load_sem.at[0]),
-        pltpu.make_async_copy(pos_ref, places.at[pl.ds(0, 3)], load_sem.at[1]),
-        pltpu.make_async_copy(mult_ref, mult, load_sem.at[2]),
-        pltpu.make_async_copy(ops_ref.at[pl.ds(4, 2)], ops, load_sem.at[3]),
-    ]
-    places[...] = jnp.zeros_like(places)
-    for load in loads:
-        load.start()
     pl.semaphore_wait(barrier, len(partners) + 2)
 
     def send(src, dst, ssem, rsem, at, c):
@@ -143,6 +147,23 @@
     for k in range(3):
         spread(k, 0, 16, 1, 0)
         spread(k, 16, 16, 3, 1)
+    loads = [
+        pltpu.make_async_copy(local_hbm, local_ref, load_sem.at[4]),
+        pltpu.make_async_copy(count_hbm, count_ref, load_sem.at[5]),
+        pltpu.make_async_copy(owner_ref, asked.at[0], load_sem.at[6]),
+        pltpu.make_async_copy(box_ref, asked.at[1], load_sem.at[7]),
+        pltpu.make_async_copy(charge_ref, charges, load_sem.at[0]),
+        pltpu.make_async_copy(pos_ref, places.at[pl.ds(0, 3)], load_sem.at[1]),
+        pltpu.make_async_copy(mult_ref, mult, load_sem.at[2]),
+    ]
+    places[...] = jnp.zeros_like(places)
+    for load in loads:
+        load.start()
+    for t in range(8):
+        for (_, _, c0, cols), start in zip(PARTS[3:], STARTS):
+            pltpu.make_async_copy(
+                ops_ref.at[16 + t, pl.ds(c0, cols)], ops.at[t // 4, pl.ds(start + t % 4 * cols, cols)], load_sem.at[3]
+            ).start()
     loads[2].wait()
     loads[3].wait()
     rows = 256
@@ -284,7 +305,7 @@
                 kernel_tiles.append(jnp.where((o >= -1) & (o <= 1), value, 0.0))
             high, low = split(jnp.concatenate(kernel_tiles, 0))
             window = shifted[:, pl.ds(pl.multiple_of(i * 128, 128), 256)]
-            potential_ref[:, tile(i)] = dot(window, high) + dot(window, low)
+            potential_ref[:, tile(i)] = jnp.where(present(i), dot(window, high) + dot(window, low), 0.0)
             return 0
 
         lax.fori_loop(0, 16, pair, 0)
@@ -308,6 +329,7 @@
                     old, new = new, 2.0 * u * new - old
                     value = value + factors[k] * new
                 weights.append((2.0 * value - 1.0) / ORDER)
+            weights[2] = jnp.where(present(i), weights[2], 0.0)
             for m1 in range(ORDER):
                 parts = [(weights[0][m1 : m1 + 1] * weights[1][m2 : m2 + 1]) * weights[2] for m2 in range(ORDER)]
                 high, low = split(jnp.concatenate(parts, 0))
@@ -319,7 +341,7 @@
 
     def load_op(t):
         return pltpu.make_async_copy(
-            ops_ref.at[t // 4, pl.ds(t % 4 * 512, 512)], stream.at[t % 2], stream_sem.at[t % 2]
+            ops_ref.at[t], stream.at[t % 2], stream_sem.at[t % 2]
         )
 
     def local_type(t):
@@ -339,36 +361,53 @@
 
         lax.fori_loop(0, 4, group, 0)
 
-    def remote_rows(parts):
-        r0 = PARTS[parts[0]][1]
-        for k in parts:
-            drain(finals[k].at[pl.ds(0, 224)], f_recv.at[k])
-            drain(finals[k].at[pl.ds(0, 32)], f_own.at[k])
-
-        def one(t, _):
-            for k in parts:
-                order, _, c0, cols = PARTS[k]
-                for half in range(4):
-                    for b in range(32):
-                        at = pl.ds(half * 512 + c0, cols)
-                        lhs[b * 16 : b * 16 + 16, at] = finals[k][slot_s[order, (4 * t + half) * 32 + b]]
-            total[:, r0 : r0 + ROWS, :] += dot(lhs[...], ops[t]).reshape(32, ROWS, 512)
+    def arrived(k):
+        drain(finals[k].at[pl.ds(0, 224)], f_recv.at[k])
+        drain(finals[k].at[pl.ds(0, 32)], f_own.at[k])
+
+    def remote_rows(k):
+        order, r0, _, _ = PARTS[k]
+        arrived(k)
+
+        def one(half, _):
+            for t in range(4):
+                for b in range(32):
+                    block = finals[k][slot_s[order, (4 * half + t) * 32 + b]]
+                    for (_, _, c0, cols), start in zip(PARTS[3:], STARTS):
+                        lhs[b * 16 : b * 16 + 16, start + t * cols : start + (t + 1) * cols] = block[:, c0 : c0 + cols]
+            total[:, r0 : r0 + ROWS, :] += dot(lhs[...], ops[half]).reshape(32, ROWS, 512)
             return 0
 
         lax.fori_loop(0, 2, one, 0)
 
-    def far_rows(r0, count):
-        def pair(i, _):
-            value = total[pl.ds(2 * i, 2), r0 : r0 + count, :].reshape(2 * count, 512)
-            high, low = split(value)
-            both = dot(jnp.concatenate([high, low], 0), tables[i])
-            summed = (both[: 2 * count, 0:128] + both[: 2 * count, 128:256]) + (both[2 * count :, 0:128] + both[2 * count :, 128:256])
-            far = jnp.where(second, summed[count:], summed[:count])
-            near = potential_ref[r0 : r0 + count, tile(i)]
-            potential_ref[r0 : r0 + count, tile(i)] = jnp.where(present(i), near + far, 0.0)
+    def fetch(k, half, t, b):
+        return finals[k][slot_s[PARTS[k][0], (4 * half + t) * 32 + b]]
+
+    def add_last(value):
+        total[:, 48:64, :] += value.reshape(32, ROWS, 512)
+
+    def last_rows_first_part():
+        arrived(3)
+
+        def one(half, _):
+            for t in range(4):
+                for b in range(32):
+                    lhs[b * 16 : b * 16 + 16, t * 128 : t * 128 + 128] = fetch(3, half, t, b)
+            add_last(dot(lhs[:, 0:512], ops[half, 0:512]))
             return 0
 
-        lax.fori_loop(0, 16, pair, 0, unroll=8)
+        lax.fori_loop(0, 2, one, 0)
+
+    def last_rows_other_parts():
+        arrived(4)
+        arrived(5)
+        for half in range(2):
+            for t in range(4):
+                for b in range(32):
+                    rows16, at = slice(b * 16, b * 16 + 16), half * 1536 + t * 128
+                    last[rows16, at : at + 128] = fetch(4, half, t, b)
+                    at = half * 1536 + 512 + t * 256
+                    last[rows16, at : at + 256] = fetch(5, half, t, b)
 
     load_op(0).start()
     for k in range(3):
@@ -389,26 +428,50 @@
         pack(k, (1, 3, 2, 0))
     t = 4
     for ks in ((0, 1, 2), (3, 4, 5)):
-        for step in (0, 1, 3, 2):
+        for step in (0, 2, 1, 3):
             for k in ks:
                 forward(k, step)
             if t < 16:
                 local_type(t)
                 local_type(t + 1)
                 t += 2
-    loads[7].wait()
+    drain(ops, load_sem.at[3])
     to_slots.wait()
     for k in range(3):
-        remote_rows((k,))
-    far_rows(0, 48)
-    remote_rows((3, 4, 5))
-    far_rows(48, 16)
+        remote_rows(k)
+    add_far(total, 0, 48, tables, potential_ref)
+    last_rows_first_part()
+    last_rows_other_parts()
     for k in range(6):
         drain(finals[k].at[pl.ds(0, 224)], f_send.at[k])
         drain(packed[k].at[pl.ds(0, 3)], s_send.at[k])
         drain(gathered[k].at[pl.ds(0, 96)], g_send.at[k])
     drain(ask_v.at[pl.ds(0, 7)], ask_send.at[0])
     drain(ask_v.at[pl.ds(0, 66)], ask_send.at[1])
+
+
+def finish_kernel(
+    expansion_ref, potential_ref, tables, ops, last, expansion_out, potential_out, rows, potentials, sems
+):
+    copies = [
+        pltpu.make_async_copy(
+            expansion_ref.at[pl.ds(i * 8, 8), pl.ds(0, 48)], expansion_out.at[pl.ds(i * 8, 8), pl.ds(0, 48)], sems.at[i]
+        )
+        for i in range(4)
+    ]
+    copies.append(pltpu.make_async_copy(potential_ref.at[pl.ds(0, 48)], potential_out.at[pl.ds(0, 48)], sems.at[4]))
+    for copy in copies:
+        copy.start()
+    value = dot(last[:, 0:1536], ops[0, 512:2048]) + dot(last[:, 1536:3072], ops[1, 512:2048])
+    rows[...] = expansion_ref[:, 48:64, :] + value.reshape(32, ROWS, 512)
+    copies.append(pltpu.make_async_copy(rows, expansion_out.at[:, pl.ds(48, 16)], sems.at[5]))
+    copies[-1].start()
+    potentials[...] = potential_ref[48:64, :]
+    add_far(rows, 0, ROWS, tables, potentials)
+    copies.append(pltpu.make_async_copy(potentials, potential_out.at[pl.ds(48, 16)], sems.at[6]))
+    copies[-1].start()
+    for copy in copies:
+        copy.wait()
 
 
 def on_device(
@@ -423,10 +486,13 @@
         out_shape=[
             pltpu.VMEM((32, 64, 512), f32),
             pltpu.VMEM((64, 2048), f32),
+            pltpu.VMEM((16, 512, 256), bf16),
+            pltpu.VMEM((2, 2048, 512), bf16),
+            pltpu.VMEM((512, 3072), bf16),
         ]
         + [jax.ShapeDtypeStruct((4, 64, ROWS, part[3]), bf16) for part in PARTS],
         in_specs=[any_space] * 8,
-        out_specs=[vmem, vmem] + [any_space] * 6,
+        out_specs=[vmem] * 5 + [any_space] * 6,
         scratch_shapes=[pltpu.VMEM((128, ROWS, part[3]), bf16) for part in PARTS]
         + [pltpu.VMEM((4, 64, ROWS, part[3]), bf16) for part in PARTS]
         + [pltpu.VMEM((256, ROWS, part[3]), bf16) for part in PARTS]
@@ -436,14 +502,12 @@
             pltpu.VMEM((8, 256), i32),
             pltpu.SMEM((8, 256), i32),
             pltpu.VMEM((32, 64, 512), bf16),
-            pltpu.VMEM((2, 2048, 512), bf16),
             pltpu.VMEM((2, 512, 512), bf16),
             pltpu.VMEM((512, 2048), bf16),
             pltpu.VMEM((64, 2048), bf16),
             pltpu.VMEM((8, 2048), f32),
             pltpu.VMEM((64, 2176), bf16),
             pltpu.VMEM((2176, 8), f32),
-            pltpu.VMEM((16, 512, 256), bf16),
             pltpu.VMEM((2, 72, 128), f32),
             pltpu.VMEM((2, 72, 128), f32),
             pltpu.VMEM((2, 2, 128), i32),
@@ -452,9 +516,17 @@
             dma((2,)), dma((2,)), dma((2,)), dma((6,)), dma((6, 3)), dma((6,)), dma((6,)), dma((6, 4)), dma((6,)), dma((6,)), dma((6,)),
             dma((8,)), dma((2,)), dma((2,)), dma((2,)),
         ],
-        compiler_params=pltpu.CompilerParams(collective_id=0, has_side_effects=True, vmem_limit_bytes=57 * 2**20),
-    )(remote_owner.reshape(2, 128), remote_box.reshape(2, 128), local_source, leaf_count, multipoles, translations.reshape(6, 2048, 512), charges, positions)
-    return results[0], results[1]
+        compiler_params=pltpu.CompilerParams(collective_id=0, has_side_effects=True, vmem_limit_bytes=48 * 2**20),
+    )(remote_owner.reshape(2, 128), remote_box.reshape(2, 128), local_source, leaf_count, multipoles, translations, charges, positions)
+    held = [pltpu.with_memory_space_constraint(value, pltpu.VMEM) for value in results[:5]]
+    return pl.pallas_call(
+        finish_kernel,
+        out_shape=[jax.ShapeDtypeStruct((32, 64, 512), f32), jax.ShapeDtypeStruct((64, 2048), f32)],
+        in_specs=[vmem] * 5,
+        out_specs=[any_space] * 2,
+        scratch_shapes=[pltpu.VMEM((32, ROWS, 512), f32), pltpu.VMEM((ROWS, 2048), f32), dma((7,))],
+        compiler_params=pltpu.CompilerParams(vmem_limit_bytes=4 * 2**20),
+    )(*held)
 
 
 def solution(mesh):

time: 165 us -> 163 us (0.988)
  local copies, waits for them, and re-layouts: 2.81 us -> 0 us
    pallas_call x0 -> x1, Pallas kernels: none -> 3.62 us  [on_device(): pl.pallas_call(finish_kernel, out_shape=[jax.ShapeDtypeStruct((32, 64, 51...]
    pallas_call x1, Pallas kernels: 161 us -> 158 us  [on_device(): pl.pallas_call(whole_kernel, out_shape=[pltpu.VMEM((32, 64, 512), f32), p...]
    unnamed x2 -> x0, local copies, waits for them, and re-layouts: 2.81 us -> none
where the time goes in v5:
time: 163 us
  Pallas kernels  162 us (99%)
    pallas_call x1, Pallas kernels, on_device(): pl.pallas_call(whole_kernel, out_shape=[pltpu.VMEM((32, 64, 512), f32), p...  158 us
    pallas_call x1, Pallas kernels, on_device(): pl.pallas_call(finish_kernel, out_shape=[jax.ShapeDtypeStruct((32, 64, 51...  3.62 us

profile of v5, /device:TPU:1, one launch (start us, length us, event | category | flops | bytes accessed | tf_op | source)
XLA Modules:
  0.0 162.6 jit_solution(874627298773797399)
XLA Ops:
  0.6 158.3 %shard_map.95 = (f32[32,64,512]{2,1,0:T(8,128)S(1)}, f32[64,2048]{1,0:T(8,128)S(1)}, bf16[16,512,256]{2,1,0:T(8,128)(2,1)S(1)}, bf16[2,2048,512]{2,1,0:T(8,128)(...) custom-call(s32[2,128]{1,0:T(2,128)} %bitcast.2, ...), custom_call_target="tpu_custom_call" | custom-call | tf_op jit(solution)/shard_map/pallas_call | solution.py:484
  158.9 3.6 %shard_map.96 = (f32[32,64,512]{2,1,0:T(8,128)}, f32[64,2048]{1,0:T(8,128)}) custom-call(f32[32,64,512]{2,1,0:T(8,128)S(1)} %get-tuple-element.7.expansion_ref, f32[64,2048]{1,0:T(8,128)S(1)} %get-tuple-element.8.potential_ref, bf16[16,512,256]{2,1,0:T(8,128)(2,1)S(1)} %get-tuple-element.9.tables, bf16[2,2048,512]{2,1,0:T(8,128)(2,1)S(1)} %get-tuple-element.10.ops, ...), custom_call_target="tpu_custom_call" | custom-call | tf_op jit(solution)/shard_map/pallas_call | solution.py:522

commit v6 on v5

--- a/solution.py
+++ b/solution.py
@@ -257,7 +257,7 @@
         if step:
             drain(relay[k].at[came[p]], s_recv.at[k, came[p]])
         slot = ((came[p] * 4 + me[q]) * 2 + core) * 8
-        for hop in (1, 3, 2, 0):
+        for hop in (2, 1, 3, 0):
             for c in (core, 1 - core):
                 to = moved(me, q, hop)
                 piece = src.at[came[p], pl.ds((to[q] * 2 + c) * 8, 8)]
@@ -399,15 +399,13 @@
         lax.fori_loop(0, 2, one, 0)
 
     def last_rows_other_parts():
-        arrived(4)
-        arrived(5)
-        for half in range(2):
-            for t in range(4):
-                for b in range(32):
-                    rows16, at = slice(b * 16, b * 16 + 16), half * 1536 + t * 128
-                    last[rows16, at : at + 128] = fetch(4, half, t, b)
-                    at = half * 1536 + 512 + t * 256
-                    last[rows16, at : at + 256] = fetch(5, half, t, b)
+        for k, first, cols in ((4, 0, 128), (5, 512, 256)):
+            arrived(k)
+            for half in range(2):
+                for t in range(4):
+                    at = first + t * cols
+                    for b in range(32):
+                        last[half, b * 16 : b * 16 + 16, at : at + cols] = fetch(k, half, t, b)
 
     load_op(0).start()
     for k in range(3):
@@ -462,8 +460,13 @@
     copies.append(pltpu.make_async_copy(potential_ref.at[pl.ds(0, 48)], potential_out.at[pl.ds(0, 48)], sems.at[4]))
     for copy in copies:
         copy.start()
-    value = dot(last[:, 0:1536], ops[0, 512:2048]) + dot(last[:, 1536:3072], ops[1, 512:2048])
-    rows[...] = expansion_ref[:, 48:64, :] + value.reshape(32, ROWS, 512)
+    rows[...] = expansion_ref[:, 48:64, :]
+
+    def one(half, _):
+        rows[...] += dot(last[half], ops[half, 512:2048]).reshape(32, ROWS, 512)
+        return 0
+
+    lax.fori_loop(0, 2, one, 0)
     copies.append(pltpu.make_async_copy(rows, expansion_out.at[:, pl.ds(48, 16)], sems.at[5]))
     copies[-1].start()
     potentials[...] = potential_ref[48:64, :]
@@ -488,7 +491,7 @@
             pltpu.VMEM((64, 2048), f32),
             pltpu.VMEM((16, 512, 256), bf16),
             pltpu.VMEM((2, 2048, 512), bf16),
-            pltpu.VMEM((512, 3072), bf16),
+            pltpu.VMEM((2, 512, 1536), bf16),
         ]
         + [jax.ShapeDtypeStruct((4, 64, ROWS, part[3]), bf16) for part in PARTS],
         in_specs=[any_space] * 8,

time: 163 us -> 163 us (level)
  no operation moved by 1% of the time
where the time goes in v6:
time: 163 us; the launch traced here: 162 us
  Pallas kernels  162 us (99%)
    pallas_call x1, Pallas kernels, on_device(): pl.pallas_call(whole_kernel, out_shape=[pltpu.VMEM((32, 64, 512), f32), p...  158 us
    pallas_call x1, Pallas kernels, on_device(): pl.pallas_call(finish_kernel, out_shape=[jax.ShapeDtypeStruct((32, 64, 51...  3.72 us

profile of v6, /device:TPU:1, one launch (start us, length us, event | category | flops | bytes accessed | tf_op | source)
XLA Modules:
  0.0 162.4 jit_solution(13303263935656696925)
XLA Ops:
  0.6 158.0 %shard_map.95 = (f32[32,64,512]{2,1,0:T(8,128)S(1)}, f32[64,2048]{1,0:T(8,128)S(1)}, bf16[16,512,256]{2,1,0:T(8,128)(2,1)S(1)}, bf16[2,2048,512]{2,1,0:T(8,128)(...) custom-call(s32[2,128]{1,0:T(2,128)} %bitcast.2, ...), custom_call_target="tpu_custom_call" | custom-call | tf_op jit(solution)/shard_map/pallas_call | solution.py:487
  158.7 3.7 %shard_map.96 = (f32[32,64,512]{2,1,0:T(8,128)}, f32[64,2048]{1,0:T(8,128)}) custom-call(f32[32,64,512]{2,1,0:T(8,128)S(1)} %get-tuple-element.7.expansion_ref, f32[64,2048]{1,0:T(8,128)S(1)} %get-tuple-element.8.potential_ref, bf16[16,512,256]{2,1,0:T(8,128)(2,1)S(1)} %get-tuple-element.9.tables, bf16[2,2048,512]{2,1,0:T(8,128)(2,1)S(1)} %get-tuple-element.10.ops, ...), custom_call_target="tpu_custom_call" | custom-call | tf_op jit(solution)/shard_map/pallas_call | solution.py:525
